TPU v7x, 32 devices: a whole 2x2x4 slice. The times are simulated.
32 devices in a mesh: dy: 8 (over y, x, core), dx: 4 (over z).
Axes of the slice: x: 2, y: 2, z: 4, core: 2. Of those that a mesh axis runs over, the one named last changes fastest.
Arguments:
- heights: float32 [4096, 2048], P('dy', 'dx'), may hold values from -4 to 4
- albedo: float32 [4096, 2048], P('dy', 'dx'), may hold values from 0.5 to 1.5
- observed: bfloat16 [512, 384, 384], P(('dy', 'dx')), may hold values from -2 to 2
- resample: bfloat16 [512, 2, 384, 384], P(('dy', 'dx')), may hold values from -1 to 1
- exposure: float32 [4, 16], P('dx'), may hold values from -0.5 to 0.5
- sun_azimuth: float32 [4, 16], P('dx'), may hold values from -3.140625 to 3.140625
- sun_elevation: float32 [4, 16], P('dx'), may hold values from 0.02 to 0.3
- send_plan: int32 [8, 4, 4, 24], P('dy', 'dx'), may hold values from 0 to 128, as said below
- recv_plan: int32 [8, 4, 16], P('dy', 'dx'), may hold values from 0 to 23, as said below
Outputs:
- height_gradient: float32 [4096, 2048], P('dy', 'dx')
- camera_gradient: float32 [4, 16, 7], P('dx', 'dy')
Inputs may be any that keep to these rules, and one draw needn't show every extreme that they name: send_plan[s, c, :, r * 3 + j] describes slot j of the crops that the DEM tile (s, c) serves to the device (r, c): row offset and column offset of the crop's window in the tile (multiples of 128, at most 128 and 128), the image m, and 1; unused slots are all zeros. Every device is served exactly 3 crops by at least one tile. recv_plan[r, c, m] = s * 3 + j names the used slot send_plan[s, c, :, r * 3 + j] whose image is m; the values of one device are distinct.
All inputs are finite; a program needn't handle non-finite values.
Results may differ from a plain program's by a relative error of at most 0.005.
Values may be sent and summed in bfloat16 or wider, within the bound.
A program may use at most 384 MiB of HBM per device.

v0:
```python
import functools

import jax
import jax.numpy as jnp
from jax import lax
from jax.experimental import pallas as pl
from jax.experimental.pallas import tpu as pltpu
from jax.sharding import PartitionSpec as P

SMOOTHING_WEIGHT = 0.02
MESH = pl.DeviceIdType.MESH
VMEM_BYTES = 56 * 1024 * 1024


def shifted(block, axis, dim, width):
    count = lax.axis_size(axis)
    forward = [(i, i + 1) for i in range(count - 1)]
    backward = [(target, source) for source, target in forward]
    low = lax.ppermute(
        lax.slice_in_dim(block, block.shape[dim] - width, None, axis=dim), axis, forward
    )
    high = lax.ppermute(lax.slice_in_dim(block, 0, width, axis=dim), axis, backward)
    return low, high


def padded_2(block, sides, width):
    for axis, dim in sides:
        low, high = shifted(block, axis, dim, width)
        block = jnp.concatenate([low, block, high], axis=dim)
    return block


def slopes(padded):
    slope_x = (padded[1:-1, 2:] - padded[1:-1, :-2]) * 0.5
    slope_y = (padded[2:, 1:-1] - padded[:-2, 1:-1]) * 0.5
    return (slope_x, slope_y)


def laplace(padded):
    return (
        padded[:-2, 1:-1]
        + padded[2:, 1:-1]
        + padded[1:-1, :-2]
        + padded[1:-1, 2:]
        - 4.0 * padded[1:-1, 1:-1]
    )


def shading(slope_x, slope_y, albedo):
    up = albedo * lax.rsqrt(1.0 + slope_x * slope_x + slope_y * slope_y)
    return jnp.stack([-slope_x * up, -slope_y * up, up])


def sun_vectors(solar_azimuth, elevation):
    return jnp.stack(
        [
            jnp.cos(elevation) * jnp.cos(solar_azimuth),
            jnp.cos(elevation) * jnp.sin(solar_azimuth),
            jnp.sin(elevation),
        ]
    )


def bit_count(count):
    bits = count.bit_length() - 1
    assert 1 << bits == count
    return bits


def flipped(index, mask, bits):
    for bit in range(bits):
        if mask >> bit & 1:
            weight = 1 << bit
            index = index + weight * (1 - 2 * ((index // weight) % 2))
    return index


def bit_orders(bits):
    up = list(range(1, bits))
    return (up, up[::-1])


def all_masks(order):
    masks = [0]
    for bit in order:
        masks = masks + [mask | 1 << bit for mask in masks]
    return masks


def gather_kernel(n, copies, own_ref, plan_ref, out_ref, plans_ref, send, recv, psend, precv, lsem):
    bits = bit_count(n)
    me = lax.axis_index("dy")
    half = own_ref.shape[1] // 2
    barrier = pltpu.get_barrier_semaphore()
    for step in range(1, n):
        pl.semaphore_signal(
            barrier, inc=1, device_id={"dy": lax.rem(me + step, n)}, device_id_type=MESH
        )
    pl.semaphore_wait(barrier, n - 1)

    number = iter(range(copies))

    def rows(part):
        return pl.ds(part * half, half)

    def make(mask, part, bit):
        tile = flipped(me, mask, bits)
        source = own_ref if mask == 0 else out_ref.at[tile]
        c = next(number)
        return pltpu.make_async_remote_copy(
            src_ref=source.at[:, rows(part), :],
            dst_ref=out_ref.at[tile, :, rows(part), :],
            send_sem=send.at[c],
            recv_sem=recv.at[c],
            device_id={"dy": flipped(me, 1 << bit, bits)},
            device_id_type=MESH,
        )

    orders = bit_orders(bits)
    started = []
    arriving = {}

    def forward(mask, part, over):
        copy = make(mask, part, over)
        copy.start()
        started.append(copy)
        arriving[(mask | 1 << over, part)] = copy

    def later(mask, order):
        seen = [k for k, bit in enumerate(order) if mask >> bit & 1]
        return order[(max(seen) + 1 if seen else 0) :]

    for position in range(bits - 1):
        for part, order in enumerate(orders):
            forward(0, part, order[position])
    plan_copies = []
    for step in range(1, n):
        to = lax.rem(me + step, n)
        copy = pltpu.make_async_remote_copy(
            src_ref=plan_ref.at[to],
            dst_ref=plans_ref.at[me],
            send_sem=psend.at[step - 1],
            recv_sem=precv.at[step - 1],
            device_id={"dy": to},
            device_id_type=MESH,
        )
        copy.start()
        plan_copies.append(copy)
    for part in range(2):
        forward(0, part, 0)
    local = pltpu.make_async_copy(own_ref, out_ref.at[me], lsem.at[0])
    local.start()
    local_plan = pltpu.make_async_copy(plan_ref.at[me], plans_ref.at[me], lsem.at[1])
    local_plan.start()
    mask_lists = [all_masks(order)[1:] for order in orders]
    for position in range(len(mask_lists[0])):
        for part, order in enumerate(orders):
            mask = mask_lists[part][position]
            arriving[(mask, part)].wait_recv()
            for bit in later(mask, order):
                forward(mask, part, bit)
            forward(mask, part, 0)
    for (mask, part), copy in arriving.items():
        if mask & 1:
            copy.wait_recv()
    for copy in started:
        copy.wait_send()
    for copy in plan_copies:
        copy.wait()
    local.wait()
    local_plan.wait()


def gather_tiles(own, plan_by_dest, n):
    bits = bit_count(n)
    high = n // 2
    copies = 2 * (high - 1) + 2 * high
    return pl.pallas_call(
        functools.partial(gather_kernel, n, copies),
        out_shape=(
            jax.ShapeDtypeStruct((n,) + own.shape, own.dtype),
            jax.ShapeDtypeStruct(plan_by_dest.shape, plan_by_dest.dtype),
        ),
        in_specs=[pl.BlockSpec(memory_space=pl.ANY)] * 2,
        out_specs=(pl.BlockSpec(memory_space=pl.ANY),) * 2,
        scratch_shapes=[
            pltpu.SemaphoreType.DMA((copies,)),
            pltpu.SemaphoreType.DMA((copies,)),
            pltpu.SemaphoreType.DMA((n - 1,)),
            pltpu.SemaphoreType.DMA((n - 1,)),
            pltpu.SemaphoreType.DMA((2,)),
        ],
        compiler_params=pltpu.CompilerParams(collective_id=0, has_side_effects=True),
        name="gather_tiles",
    )(own, plan_by_dest)


def render_kernel(
    plans, pick, used, light, tiles_ref, mats_ref, seen_ref, grads_ref, sums_ref, total
):
    tile, slot = pl.program_id(0), pl.program_id(1)
    most = pl.num_programs(1)
    step = tile * most + slot
    size = seen_ref.shape[-1]

    @pl.when(slot == 0)
    def _():
        total[...] = jnp.zeros_like(total)

    @pl.when(used[step] == 1)
    def _():
        image = pick[step]
        rows = pl.ds(pl.multiple_of(plans[tile, 0, slot], 128), size)
        cols = pl.ds(pl.multiple_of(plans[tile, 1, slot], 128), size)
        sun_x, sun_y, sun_z = light[0, image], light[1, image], light[2, image]
        gain = light[3, image]

        def field(k):
            return tiles_ref[0, k, rows, cols].astype(jnp.float32)

        shaded = (sun_x * field(0) + sun_y * field(1) + sun_z * field(2)).astype(jnp.bfloat16)
        first = jnp.dot(mats_ref[0, 0], shaded, preferred_element_type=jnp.float32)
        predicted = gain * lax.dot_general(
            first.astype(jnp.bfloat16),
            mats_ref[0, 1],
            (((1,), (1,)), ((), ())),
            preferred_element_type=jnp.float32,
        )
        residual = predicted - seen_ref[0].astype(jnp.float32)
        weighted = (gain * residual).astype(jnp.bfloat16)
        back = lax.dot_general(
            mats_ref[0, 0], weighted, (((0,), (0,)), ((), ())), preferred_element_type=jnp.float32
        ).astype(jnp.bfloat16)
        crop_grad = jnp.dot(back, mats_ref[0, 1], preferred_element_type=jnp.float32)

        col = lax.broadcasted_iota(jnp.int32, (1, size), 1)
        row = lax.broadcasted_iota(jnp.int32, (size, 1), 0)
        last = size - 1
        right = jnp.where(col == last, predicted, pltpu.roll(predicted, last, 1))
        left = jnp.where(col == 0, predicted, pltpu.roll(predicted, 1, 1))
        below = jnp.where(row == last, predicted, pltpu.roll(predicted, last, 0))
        above = jnp.where(row == 0, predicted, pltpu.roll(predicted, 1, 0))
        col_weight = jnp.where((col == 0) | (col == last), 1.0, 0.5)
        row_weight = jnp.where((row == 0) | (row == last), 1.0, 0.5)
        row_place = (row.astype(jnp.float32) - 0.5 * (size - 1)) / size
        by_u = residual * (right - left)
        by_v = residual * ((below - above) * row_weight)
        sums_ref[image, 0:1] = col_weight * jnp.sum(by_u, axis=0, keepdims=True)
        sums_ref[image, 1:2] = col_weight * jnp.sum(by_u * row_place, axis=0, keepdims=True)
        sums_ref[image, 2:3] = jnp.sum(by_v, axis=0, keepdims=True)
        sums_ref[image, 3:4] = jnp.sum(by_v * row_place, axis=0, keepdims=True)
        sums_ref[image, 4:5] = jnp.sum(residual * predicted, axis=0, keepdims=True)
        sums_ref[image, 5:8] = jnp.zeros((3, size), jnp.float32)

        fx, fy, fz = field(0), field(1), field(2)
        along = (sun_x * fx + sun_y * fy + sun_z * fz) / (fx * fx + fy * fy + fz * fz)
        scaled = crop_grad * fz
        total[0, rows, cols] += scaled * (fx * along - sun_x)
        total[1, rows, cols] += scaled * (fy * along - sun_y)

    @pl.when(slot == most - 1)
    def _():
        grads_ref[0] = total[...].astype(grads_ref.dtype)


def render(plans, pick, used, light, tiles, resample, observed, most):
    n, _, tile_rows, tile_cols = tiles.shape
    crops, size, _ = observed.shape

    def crop_at(t, j, plans, pick, used):
        return pick[t * most + j]

    def inner(plans, pick, used, light, *refs):
        render_kernel(plans, pick, used, light, *refs)

    return pl.pallas_call(
        inner,
        out_shape=(
            jax.ShapeDtypeStruct((n, 2, tile_rows, tile_cols), jnp.bfloat16),
            jax.ShapeDtypeStruct((crops, 8, size), jnp.float32),
        ),
        grid_spec=pltpu.PrefetchScalarGridSpec(
            num_scalar_prefetch=3,
            grid=(n, most),
            in_specs=[
                pl.BlockSpec(memory_space=pltpu.SMEM),
                pl.BlockSpec((1, 3, tile_rows, tile_cols), lambda t, j, *s: (t, 0, 0, 0)),
                pl.BlockSpec((1, 2, size, size), lambda t, j, *s: (crop_at(t, j, *s), 0, 0, 0)),
                pl.BlockSpec((1, size, size), lambda t, j, *s: (crop_at(t, j, *s), 0, 0)),
            ],
            out_specs=(
                pl.BlockSpec((1, 2, tile_rows, tile_cols), lambda t, j, *s: (t, 0, 0, 0)),
                pl.BlockSpec((crops, 8, size), lambda t, j, *s: (0, 0, 0)),
            ),
            scratch_shapes=[pltpu.VMEM((2, tile_rows, tile_cols), jnp.float32)],
        ),
        compiler_params=pltpu.CompilerParams(
            dimension_semantics=("arbitrary", "arbitrary"), vmem_limit_bytes=VMEM_BYTES
        ),
        name="render",
    )(plans, pick, used, light, tiles, resample, observed)


def scatter_kernel(
    n, grads_ref, sums_ref, out_ref, camera_ref, first, later, csums, send, recv, csend, crecv
):
    bits = bit_count(n)
    me = lax.axis_index("dy")
    half = out_ref.shape[1] // 2
    barrier = pltpu.get_barrier_semaphore()
    for step in range(1, n):
        pl.semaphore_signal(
            barrier, inc=1, device_id={"dy": lax.rem(me + step, n)}, device_id_type=MESH
        )
    pl.semaphore_wait(barrier, n - 1)

    number = iter(range(send.shape[0]))
    started = []

    def push(source, target, bit):
        c = next(number)
        copy = pltpu.make_async_remote_copy(
            src_ref=source,
            dst_ref=target,
            send_sem=send.at[c],
            recv_sem=recv.at[c],
            device_id={"dy": flipped(me, 1 << bit, bits)},
            device_id_type=MESH,
        )
        copy.start()
        started.append(copy)
        return copy

    masks = [m << 1 for m in range(n // 2)][::-1]
    pair = {}
    for mask in masks:
        pair[mask] = push(grads_ref.at[flipped(me, mask + 1, bits)], first.at[mask >> 1], 0)
    camera_copies = []
    for step in range(1, n):
        to = lax.rem(me + step, n)
        copy = pltpu.make_async_remote_copy(
            src_ref=sums_ref.at[to],
            dst_ref=csums.at[step - 1],
            send_sem=csend.at[step - 1],
            recv_sem=crecv.at[step - 1],
            device_id={"dy": to},
            device_id_type=MESH,
        )
        copy.start()
        camera_copies.append(copy)

    orders = bit_orders(bits)
    places = iter(range(later.shape[0]))
    coming = {}

    def rows(part):
        return pl.ds(part * half, half)

    for mask in masks:
        pair[mask].wait_recv()
        mine = grads_ref[flipped(me, mask, bits)].astype(jnp.float32)
        both = mine + first[mask >> 1].astype(jnp.float32)
        if mask == 0:
            out_ref[...] = both
        else:
            first[mask >> 1] = both.astype(first.dtype)
            for part, order in enumerate(orders):
                if mask >> order[0] & 1:
                    at = next(places)
                    source = first.at[mask >> 1, :, rows(part), :]
                    copy = push(source, later.at[at], order[0])
                    coming[(part, mask ^ 1 << order[0])] = (copy, at)
    for stage in range(bits - 1):
        for part, order in enumerate(orders):
            landed = [(m, coming.pop((p, m))) for p, m in list(coming) if p == part]
            for mask, (copy, at) in landed:
                copy.wait_recv()
                add = later[at].astype(jnp.float32)
                if mask == 0:
                    out_ref[:, rows(part), :] += add
                else:
                    held = first[mask >> 1, :, rows(part), :].astype(jnp.float32)
                    first[mask >> 1, :, rows(part), :] = (held + add).astype(first.dtype)
                    bit = order[stage + 1]
                    if mask >> bit & 1:
                        to = next(places)
                        source = first.at[mask >> 1, :, rows(part), :]
                        sent = push(source, later.at[to], bit)
                        coming[(part, mask ^ 1 << bit)] = (sent, to)
    camera = sums_ref[me]
    for step in range(1, n):
        camera_copies[step - 1].wait()
        camera = camera + csums[step - 1]
    camera_ref[...] = camera
    for copy in started:
        copy.wait_send()


def scatter_sums(grads, sums, n):
    _, parts, tile_rows, tile_cols = grads.shape
    high = n // 2
    halves = 2 * (high - 1)
    copies = high + halves
    return pl.pallas_call(
        functools.partial(scatter_kernel, n),
        out_shape=(
            jax.ShapeDtypeStruct(grads.shape[1:], jnp.float32),
            jax.ShapeDtypeStruct(sums.shape[1:], jnp.float32),
        ),
        in_specs=[pl.BlockSpec(memory_space=pltpu.VMEM)] * 2,
        out_specs=(pl.BlockSpec(memory_space=pltpu.VMEM),) * 2,
        scratch_shapes=[
            pltpu.VMEM((high, parts, tile_rows, tile_cols), grads.dtype),
            pltpu.VMEM((halves, parts, tile_rows // 2, tile_cols), grads.dtype),
            pltpu.VMEM((n - 1,) + sums.shape[1:], jnp.float32),
            pltpu.SemaphoreType.DMA((copies,)),
            pltpu.SemaphoreType.DMA((copies,)),
            pltpu.SemaphoreType.DMA((n - 1,)),
            pltpu.SemaphoreType.DMA((n - 1,)),
        ],
        compiler_params=pltpu.CompilerParams(
            collective_id=1, has_side_effects=True, vmem_limit_bytes=VMEM_BYTES
        ),
        name="scatter_sums",
    )(grads, sums)


def per_device(
    heights, albedo, observed, resample, exposure, sun_azimuth, sun_elevation, send_plan, recv_plan
):
    n = lax.axis_size("dy")
    tile_rows, tile_cols = heights.shape
    crops, size = observed.shape[0], observed.shape[-1]
    slot_count = send_plan.shape[-1]
    most = slot_count // n
    receive = recv_plan[0, 0]
    sun_table = sun_vectors(sun_azimuth[0], sun_elevation[0])
    light = jnp.concatenate([sun_table, jnp.exp(exposure)])
    slot_ids = jnp.arange(slot_count, dtype=jnp.int32)
    reached = jnp.where(receive[None, :] <= slot_ids[:, None], receive[None, :], -1)
    pick = jnp.argmax(reached, axis=1).astype(jnp.int32)
    used = (jnp.max(reached, axis=1) == slot_ids).astype(jnp.int32)
    plan_by_dest = jnp.pad(
        send_plan[0, 0, 0:2].reshape(2, n, most).transpose(1, 0, 2),
        ((0, 0), (0, 6), (0, 128 - most)),
    )

    wide_rim = padded_2(heights, (("dy", 0), ("dx", 1)), 2)
    slope_x, slope_y = slopes(wide_rim[1:-1, 1:-1])
    fields = shading(slope_x, slope_y, albedo).astype(jnp.bfloat16)
    tiles, plans = gather_tiles(fields, plan_by_dest, n)

    lap_field = laplace(wide_rim)
    row_ids = jnp.arange(tile_rows + 2)
    col_ids = jnp.arange(tile_cols + 2)
    row_keep = ~(
        (row_ids == 0) & (lax.axis_index("dy") == 0)
        | (row_ids == tile_rows + 1) & (lax.axis_index("dy") == lax.axis_size("dy") - 1)
    )
    col_keep = ~(
        (col_ids == 0) & (lax.axis_index("dx") == 0)
        | (col_ids == tile_cols + 1) & (lax.axis_index("dx") == lax.axis_size("dx") - 1)
    )
    keep_mask = row_keep[:, None] & col_keep[None, :]
    smoothness_term = laplace(jnp.where(keep_mask, lap_field, 0.0))

    tile_grads, sums = render(plans, pick, used, light, tiles, resample, observed, most)
    grads, camera = scatter_sums(tile_grads, sums.reshape(n, crops // n, 8, size), n)

    coordinate = (jnp.arange(size, dtype=jnp.float32) - 0.5 * (size - 1)) / size
    plain = jnp.sum(camera, axis=-1)
    placed = jnp.sum(camera * coordinate, axis=-1)
    camera_model = jnp.stack(
        [
            plain[:, 0] / size,
            placed[:, 0] / size,
            plain[:, 1] / size,
            plain[:, 2] / size,
            placed[:, 2] / size,
            plain[:, 3] / size,
            plain[:, 4] / (size * size),
        ],
        axis=-1,
    )

    grad_x, grad_y = grads[0], grads[1]
    low_x, high_x = shifted(grad_x.astype(jnp.bfloat16), "dx", 1, 1)
    low_y, high_y = shifted(grad_y.astype(jnp.bfloat16), "dy", 0, 1)
    rim_x = jnp.concatenate([low_x.astype(jnp.float32), grad_x, high_x.astype(jnp.float32)], axis=1)
    rim_y = jnp.concatenate([low_y.astype(jnp.float32), grad_y, high_y.astype(jnp.float32)], axis=0)
    data_term_gradient = (rim_x[:, :-2] - rim_x[:, 2:]) * 0.5 + (rim_y[:-2] - rim_y[2:]) * 0.5
    height_gradient = data_term_gradient + SMOOTHING_WEIGHT * smoothness_term
    return (height_gradient, camera_model[None])


def solution(mesh):
    placed = (
        P("dy", "dx"),
        P("dy", "dx"),
        P(("dy", "dx"), None, None),
        P(("dy", "dx"), None, None, None),
        P("dx", None),
        P("dx", None),
        P("dx", None),
        P("dy", "dx", None, None),
        P("dy", "dx", None),
    )
    return jax.shard_map(
        per_device,
        mesh=mesh,
        in_specs=placed,
        out_specs=(P("dy", "dx"), P("dx", "dy", None)),
        check_vma=False,
    )
```

profile of v0, /device:TPU:0, one launch (start us, length us, event | category | flops | bytes accessed | tf_op | source)
XLA Modules:
  0.0 204.7 jit_solution(4333954813277575337)
XLA Ops:
  0.7 0.8 fusion.24
  1.5 1.3 collective-permute-start.1
  2.8 3.0 %collective-permute-start = (f32[2,512]{1,0:T(2,128)S(1)}, f32[2,512]{1,0:T(2,128)S(1)}, u32[]{:S(2)}, u32[]{:S(2)}) collective-permute-start(f32[2,512]{1,0:T(2,128)S(1)} %get-tuple-element.30), channel_id=1, source_target_pairs={{0,4},{4,8},{8,12},{12,16},{16,20},{20,24},{24,28},{1,5},{5,9},{9,... | collective-permute-start | bytes 12296 | tf_op jit(solution)/shard_map/ppermute | solution.py:19
  5.8 1.3 select_reduce_fusion.1
  7.1 0.7 select_reduce_fusion
  10.5 1.2 pad_maximum_fusion.9
  11.7 1.3 collective-permute-start.2
  13.0 5.6 %collective-permute-start.3 = (f32[516,2]{1,0:T(8,128)S(1)}, f32[516,2]{1,0:T(8,128)S(1)}, u32[]{:S(2)}, u32[]{:S(2)}) collective-permute-start(f32[516,2]{1,0:T(8,128)S(1)} %get-tuple-element.26), channel_id=1, source_target_pairs={{0,1},{1,2},{2,3},{4,5},{5,6},{6,7},{8,9},{9,10},{10,11},{12,13},{... | collective-permute-start | bytes 12392 | tf_op jit(solution)/shard_map/ppermute | solution.py:19
  19.9 3.5 %collective-permute-done.2 = f32[516,2]{1,0:T(8,128)S(1)} collective-permute-done((f32[516,2]{1,0:T(8,128)S(1)}, f32[516,2]{1,0:T(8,128)S(1)}, u32[]{:S(2)}, u32[]{:S(2)}) %collective-permute-start.2) | collective-permute-done | bytes 4160 | tf_op jit(solution)/shard_map/ppermute | solution.py:22
  23.3 1.7 collective-permute-done.3
  25.5 1.0 fusion.12
  26.9 1.3 pad_maximum_fusion.own_ref
  28.2 59.4 %gather_tiles.1 = (bf16[8,3,512,512]{3,2,1,0:T(8,128)(2,1)}, s32[8,8,128]{2,1,0:T(8,128)}) custom-call(bf16[3,512,512]{2,1,0:T(8,128)(2,1)} %pad_maximum_fusion.own_ref, s32[8,8,128]{2,1,0:T(8,128)} %pad.4.plan_ref), custom_call_target="tpu_custom_call" | custom-call | tf_op jit(solution)/shard_map/gather_tiles/pallas_call | solution.py:178
  87.7 46.1 %render.1 = (bf16[8,2,512,512]{3,2,1,0:T(8,128)(2,1)}, f32[16,8,384]{2,1,0:T(8,128)}) custom-call(s32[8,8,128]{2,1,0:T(8,128)} %get-tuple-element.9.plans, s32[24]{0:T(128)} %get-tuple-element.10.pick, s32[24]{0:T(128)} %compare_convert_fusion.used, f32[4,16]{1,0:T(4,128)} %pad_maximum_fusion.12.light, bf16[8,3,512,512]{3,2,1,0:T(8,128)(2,1)} %get-tuple-element.11.refs_0_, ...), custom_call_target="tpu_custom_call" | custom-call | tf_op jit(solution)/shard_map/render/pallas_call | solution.py:276
  133.8 48.4 %scatter_sums.1 = (f32[2,512,512]{2,1,0:T(8,128)}, f32[2,8,384]{2,1,0:T(8,128)}) custom-call(bf16[8,2,512,512]{3,2,1,0:T(8,128)(2,1)} %get-tuple-element.12.grads_ref, f32[8,2,8,384]{3,2,1,0:T(8,128)} %bitcast.20), custom_call_target="tpu_custom_call" | custom-call | tf_op jit(solution)/shard_map/scatter_sums/pallas_call | solution.py:404
  182.2 1.8 fusion.22
  184.4 1.5 slice_bitcast_fusion.1
  185.9 1.3 collective-permute-start.7
  187.2 3.0 %collective-permute-start.6 = (bf16[1,512]{1,0:T(2,128)(2,1)S(1)}, bf16[1,512]{1,0:T(2,128)(2,1)S(1)}, u32[]{:S(2)}, u32[]{:S(2)}) collective-permute-start(bf16[1,512]{1,0:T(2,128)(2,1)S(1)} %get-tuple-element.34), channel_id=1, source_target_pairs={{0,4},{4,8},{8,12},{12,16},{16,20},{20,24},{24,28},{1,5},{5,9},{9,... | collective-permute-start | bytes 3080 | tf_op jit(solution)/shard_map/ppermute | solution.py:19
  190.3 1.3 collective-permute-start.5
  191.6 4.6 %collective-permute-start.4 = (bf16[512,1]{1,0:T(8,128)(2,1)S(1)}, bf16[512,1]{1,0:T(8,128)(2,1)S(1)}, u32[]{:S(2)}, u32[]{:S(2)}) collective-permute-start(bf16[512,1]{1,0:T(8,128)(2,1)S(1)} %get-tuple-element.32), channel_id=1, source_target_pairs={{0,1},{1,2},{2,3},{4,5},{5,6},{6,7},{8,9},{9,10},{10,11},{12,13},{... | collective-permute-start | bytes 3080 | tf_op jit(solution)/shard_map/ppermute | solution.py:19
  196.8 0.8 copy-done.2
  197.6 1.3 fusion.1
  199.8 4.9 %fusion.4 = f32[512,512]{1,0:T(8,128)} fusion(f32[514,514]{1,0:T(8,128)S(1)} %fusion.1, f32[1,512]{1,0:T(1,128)S(1)} %convert_element_type.28, f32[512,512]{1,0:T(8,128)} %get-tuple-element.21, f32[1,512]{1,0:T(1,128)S(1)} %convert_element_type.27, f32[512,1]{1,0:T(8,128)S(1)} %convert_element_type.25, f32[512,512]{1,0:T(8,128)} %get-tuple-element.20, ...), kind=kLoop, calls=%fused_computation.13 | loop fusion | flops 3932160 | bytes 8396800 | tf_op jit(solution)/shard_map/add | solution.py:492
  (41 shorter events, 6.7 us)
Async XLA Ops:
  0.6 24.4 %copy-start = (f32[512,512]{1,0:T(8,128)S(1)}, f32[512,512]{1,0:T(8,128)}, u32[]{:S(2)}) copy-start(f32[512,512]{1,0:T(8,128)} %param.9) | copy-start | bytes 3145732
  0.6 18.5 %slice-start = ((s32[1,1,4,24]{3,2,1,0:T(4,128)}), s32[1,1,2,24]{3,2,1,0:T(2,128)S(1)}, s32[]{:S(2)}) async-start(s32[1,1,4,24]{3,2,1,0:T(4,128)} %param.16), calls=%async_computation | async-start | bytes 2048 | tf_op jit(solution)/shard_map/slice | solution.py:444
  1.5 9.0 %collective-permute-start.1 = (f32[2,512]{1,0:T(2,128)S(1)}, f32[2,512]{1,0:T(2,128)S(1)}, u32[]{:S(2)}, u32[]{:S(2)}) collective-permute-start(f32[2,512]{1,0:T(2,128)S(1)} %get-tuple-element.31), channel_id=1, source_target_pairs={{4,0},{8,4},{12,8},{16,12},{20,16},{24,20},{28,24},{5,1},{9,5},{13... | collective-permute-start | bytes 12296 | tf_op jit(solution)/shard_map/ppermute | solution.py:22
  2.8 7.7 %collective-permute-start = (f32[2,512]{1,0:T(2,128)S(1)}, f32[2,512]{1,0:T(2,128)S(1)}, u32[]{:S(2)}, u32[]{:S(2)}) collective-permute-start(f32[2,512]{1,0:T(2,128)S(1)} %get-tuple-element.30), channel_id=1, source_target_pairs={{0,4},{4,8},{8,12},{12,16},{16,20},{20,24},{24,28},{1,5},{5,9},{9,... | collective-permute-start | bytes 12296 | tf_op jit(solution)/shard_map/ppermute | solution.py:19
  11.7 11.7 %collective-permute-start.2 = (f32[516,2]{1,0:T(8,128)S(1)}, f32[516,2]{1,0:T(8,128)S(1)}, u32[]{:S(2)}, u32[]{:S(2)}) collective-permute-start(f32[516,2]{1,0:T(8,128)S(1)} %get-tuple-element.27), channel_id=1, source_target_pairs={{1,0},{2,1},{3,2},{5,4},{6,5},{7,6},{9,8},{10,9},{11,10},{13,12},{... | collective-permute-start | bytes 12392 | tf_op jit(solution)/shard_map/ppermute | solution.py:22
  13.0 12.0 %collective-permute-start.3 = (f32[516,2]{1,0:T(8,128)S(1)}, f32[516,2]{1,0:T(8,128)S(1)}, u32[]{:S(2)}, u32[]{:S(2)}) collective-permute-start(f32[516,2]{1,0:T(8,128)S(1)} %get-tuple-element.26), channel_id=1, source_target_pairs={{0,1},{1,2},{2,3},{4,5},{5,6},{6,7},{8,9},{9,10},{10,11},{12,13},{... | collective-permute-start | bytes 12392 | tf_op jit(solution)/shard_map/ppermute | solution.py:19
  19.9 5.6 %copy-start.4 = (f32[512,512]{1,0:T(8,128)S(1)}, f32[512,512]{1,0:T(8,128)}, u32[]{:S(2)}) copy-start(f32[512,512]{1,0:T(8,128)} %param.10) | copy-start | bytes 3145732
  25.5 1.1 copy-start.1
  182.2 2.2 %copy-start.3 = (f32[2,512,512]{2,1,0:T(8,128)S(1)}, f32[2,512,512]{2,1,0:T(8,128)}, u32[]{:S(2)}) copy-start(f32[2,512,512]{2,1,0:T(8,128)} %get-tuple-element.14) | copy-start | bytes 6291460
  184.4 11.8 %copy-start.5 = (f32[2,8,384]{2,1,0:T(8,128)S(1)}, f32[2,8,384]{2,1,0:T(8,128)}, u32[]{:S(2)}) copy-start(f32[2,8,384]{2,1,0:T(8,128)} %get-tuple-element.15) | copy-start | bytes 73732
  185.9 13.8 %collective-permute-start.7 = (bf16[1,512]{1,0:T(2,128)(2,1)S(1)}, bf16[1,512]{1,0:T(2,128)(2,1)S(1)}, u32[]{:S(2)}, u32[]{:S(2)}) collective-permute-start(bf16[1,512]{1,0:T(2,128)(2,1)S(1)} %get-tuple-element.35), channel_id=1, source_target_pairs={{4,0},{8,4},{12,8},{16,12},{20,16},{24,20},{28,24},{5,1},{9,5},{13... | collective-permute-start | bytes 3080 | tf_op jit(solution)/shard_map/ppermute | solution.py:22
  187.2 12.5 %collective-permute-start.6 = (bf16[1,512]{1,0:T(2,128)(2,1)S(1)}, bf16[1,512]{1,0:T(2,128)(2,1)S(1)}, u32[]{:S(2)}, u32[]{:S(2)}) collective-permute-start(bf16[1,512]{1,0:T(2,128)(2,1)S(1)} %get-tuple-element.34), channel_id=1, source_target_pairs={{0,4},{4,8},{8,12},{12,16},{16,20},{20,24},{24,28},{1,5},{5,9},{9,... | collective-permute-start | bytes 3080 | tf_op jit(solution)/shard_map/ppermute | solution.py:19
  190.3 9.3 %collective-permute-start.5 = (bf16[512,1]{1,0:T(8,128)(2,1)S(1)}, bf16[512,1]{1,0:T(8,128)(2,1)S(1)}, u32[]{:S(2)}, u32[]{:S(2)}) collective-permute-start(bf16[512,1]{1,0:T(8,128)(2,1)S(1)} %get-tuple-element.33), channel_id=1, source_target_pairs={{1,0},{2,1},{3,2},{5,4},{6,5},{7,6},{9,8},{10,9},{11,10},{13,12},{... | collective-permute-start | bytes 3080 | tf_op jit(solution)/shard_map/ppermute | solution.py:22
  191.6 8.1 %collective-permute-start.4 = (bf16[512,1]{1,0:T(8,128)(2,1)S(1)}, bf16[512,1]{1,0:T(8,128)(2,1)S(1)}, u32[]{:S(2)}, u32[]{:S(2)}) collective-permute-start(bf16[512,1]{1,0:T(8,128)(2,1)S(1)} %get-tuple-element.32), channel_id=1, source_target_pairs={{0,1},{1,2},{2,3},{4,5},{5,6},{6,7},{8,9},{9,10},{10,11},{12,13},{... | collective-permute-start | bytes 3080 | tf_op jit(solution)/shard_map/ppermute | solution.py:19
  196.3 1.3 copy-start.2
where the time goes:
time: 205 us
  Pallas kernels  154 us (75%)
  starting transfers between devices  21.3 us (10%)
  other arithmetic  15.1 us (7%)
  local copies, waits for them, and re-layouts  8.29 us (4%)
  waiting for transfers between devices  5.15 us (3%)
    pallas_call x1, Pallas kernels, gather_tiles(): pl.pallas_call(functools.partial(gather_kernel, n, copies), out_shape=(ja...  59.4 us
    pallas_call x1, Pallas kernels, scatter_sums(): pl.pallas_call(functools.partial(scatter_kernel, n), out_shape=(jax.Shape...  48.4 us
    pallas_call x1, Pallas kernels, render(): pl.pallas_call(inner, out_shape=(jax.ShapeDtypeStruct((n, 2, tile_rows, t...  46.1 us
    ppermute x4, starting transfers between devices, shifted(): lax.ppermute(lax.slice_in_dim(block, block.shape[dim] - width, None, axis...  16.2 us
    ppermute x4, starting transfers between devices, shifted(): lax.ppermute(lax.slice_in_dim(block, 0, width, axis=dim), axis, backward)  5.15 us
    add x1, other arithmetic, per_device(): height_gradient = data_term_gradient + SMOOTHING_WEIGHT * smoothness_term  4.93 us
  transfers between devices with their start and end apart: 8, of which 2 were waited for; matrix products, arithmetic and copies ran while one was open for 4% of the time, Pallas kernels for 0%

commit v1 on v0

--- a/solution.py
+++ b/solution.py
@@ -10,45 +10,6 @@
 SMOOTHING_WEIGHT = 0.02
 MESH = pl.DeviceIdType.MESH
 VMEM_BYTES = 56 * 1024 * 1024
-
-
-def shifted(block, axis, dim, width):
-    count = lax.axis_size(axis)
-    forward = [(i, i + 1) for i in range(count - 1)]
-    backward = [(target, source) for source, target in forward]
-    low = lax.ppermute(
-        lax.slice_in_dim(block, block.shape[dim] - width, None, axis=dim), axis, forward
-    )
-    high = lax.ppermute(lax.slice_in_dim(block, 0, width, axis=dim), axis, backward)
-    return low, high
-
-
-def padded_2(block, sides, width):
-    for axis, dim in sides:
-        low, high = shifted(block, axis, dim, width)
-        block = jnp.concatenate([low, block, high], axis=dim)
-    return block
-
-
-def slopes(padded):
-    slope_x = (padded[1:-1, 2:] - padded[1:-1, :-2]) * 0.5
-    slope_y = (padded[2:, 1:-1] - padded[:-2, 1:-1]) * 0.5
-    return (slope_x, slope_y)
-
-
-def laplace(padded):
-    return (
-        padded[:-2, 1:-1]
-        + padded[2:, 1:-1]
-        + padded[1:-1, :-2]
-        + padded[1:-1, 2:]
-        - 4.0 * padded[1:-1, 1:-1]
-    )
-
-
-def shading(slope_x, slope_y, albedo):
-    up = albedo * lax.rsqrt(1.0 + slope_x * slope_x + slope_y * slope_y)
-    return jnp.stack([-slope_x * up, -slope_y * up, up])
 
 
 def sun_vectors(solar_azimuth, elevation):
@@ -87,16 +48,139 @@
     return masks
 
 
-def gather_kernel(n, copies, own_ref, plan_ref, out_ref, plans_ref, send, recv, psend, precv, lsem):
-    bits = bit_count(n)
-    me = lax.axis_index("dy")
-    half = own_ref.shape[1] // 2
+def columns_as_rows(block, low):
+    width = block.shape[1]
+    if low:
+        return jnp.transpose(block[:, :128])[:8]
+    return jnp.transpose(block[:, width - 128 :])[120:]
+
+
+def rows_as_columns(rows, low):
+    empty = jnp.zeros((120, rows.shape[1]), rows.dtype)
+    parts = [empty, rows] if low else [rows, empty]
+    return jnp.transpose(jnp.concatenate(parts, axis=0))
+
+
+def greet(n, n_dx, corners):
+    me, across = lax.axis_index("dy"), lax.axis_index("dx")
     barrier = pltpu.get_barrier_semaphore()
     for step in range(1, n):
         pl.semaphore_signal(
             barrier, inc=1, device_id={"dy": lax.rem(me + step, n)}, device_id_type=MESH
         )
-    pl.semaphore_wait(barrier, n - 1)
+    for side in (1, n_dx - 1):
+        for up in (0, 1, n - 1) if corners else (0,):
+            pl.semaphore_signal(
+                barrier,
+                inc=1,
+                device_id={"dy": lax.rem(me + up, n), "dx": lax.rem(across + side, n_dx)},
+                device_id_type=MESH,
+            )
+    pl.semaphore_wait(barrier, n - 1 + (6 if corners else 2))
+
+
+def gather_kernel(
+    n,
+    n_dx,
+    copies,
+    heights_ref,
+    albedo_ref,
+    plan_ref,
+    out_ref,
+    plans_ref,
+    smooth_ref,
+    own_ref,
+    edges,
+    row_rim,
+    col_rim,
+    corner_rim,
+    wide,
+    send,
+    recv,
+    psend,
+    precv,
+    hsend,
+    hrecv,
+    lsem,
+):
+    bits = bit_count(n)
+    me, across = lax.axis_index("dy"), lax.axis_index("dx")
+    tile_rows, tile_cols = heights_ref.shape
+    half = tile_rows // 2
+    heights = heights_ref[...]
+    edges[0] = columns_as_rows(heights, True)
+    edges[1] = columns_as_rows(heights, False)
+    greet(n, n_dx, True)
+
+    row_parts = (pl.ds(0, 8), pl.ds(tile_rows - 8, 8))
+    col_parts = (pl.ds(0, 128), pl.ds(tile_cols - 128, 128))
+    row_to = (lax.rem(me + n - 1, n), lax.rem(me + 1, n))
+    col_to = (lax.rem(across + n_dx - 1, n_dx), lax.rem(across + 1, n_dx))
+    halos = []
+
+    def halo(source, target, device):
+        c = len(halos)
+        copy = pltpu.make_async_remote_copy(
+            src_ref=source,
+            dst_ref=target,
+            send_sem=hsend.at[c],
+            recv_sem=hrecv.at[c],
+            device_id=device,
+            device_id_type=MESH,
+        )
+        copy.start()
+        halos.append(copy)
+
+    for up in range(2):
+        halo(edges.at[up], col_rim.at[up], {"dx": col_to[up]})
+    for up in range(2):
+        halo(heights_ref.at[row_parts[up]], row_rim.at[up], {"dy": row_to[up]})
+    for up in range(2):
+        for right in range(2):
+            halo(
+                heights_ref.at[row_parts[up], col_parts[right]],
+                corner_rim.at[up * 2 + right],
+                {"dy": row_to[up], "dx": col_to[right]},
+            )
+    for copy in halos:
+        copy.wait_recv()
+
+    top, bottom = row_rim[1], row_rim[0]
+    wide[...] = jnp.zeros_like(wide)
+    inner_rows, inner_cols = pl.ds(8, tile_rows), pl.ds(128, tile_cols)
+    wide[inner_rows, inner_cols] = heights
+    wide[0:8, inner_cols] = jnp.where(me > 0, top, 0.0)
+    wide[pl.ds(8 + tile_rows, 8), inner_cols] = jnp.where(me < n - 1, bottom, 0.0)
+    wide[inner_rows, 0:128] = jnp.where(across > 0, rows_as_columns(col_rim[1], True), 0.0)
+    wide[inner_rows, pl.ds(128 + tile_cols, 128)] = jnp.where(
+        across < n_dx - 1, rows_as_columns(col_rim[0], False), 0.0
+    )
+    for up in range(2):
+        for right in range(2):
+            inside = (me > 0 if up else me < n - 1) & (across > 0 if right else across < n_dx - 1)
+            wide[
+                pl.ds(0 if up else 8 + tile_rows, 8), pl.ds(0 if right else 128 + tile_cols, 128)
+            ] = jnp.where(inside, corner_rim[up * 2 + right], 0.0)
+
+    def inner(block):
+        return block[8 : 8 + tile_rows, 128 : 128 + tile_cols]
+
+    def around(block):
+        rows_all, cols_all = block.shape
+        return (
+            pltpu.roll(block, 1, 0),
+            pltpu.roll(block, rows_all - 1, 0),
+            pltpu.roll(block, 1, 1),
+            pltpu.roll(block, cols_all - 1, 1),
+        )
+
+    above, below, left, right = around(wide[...])
+    slope_x = inner(right - left) * 0.5
+    slope_y = inner(below - above) * 0.5
+    up = albedo_ref[...] * lax.rsqrt(1.0 + slope_x * slope_x + slope_y * slope_y)
+    own_ref[0] = (-slope_x * up).astype(own_ref.dtype)
+    own_ref[1] = (-slope_y * up).astype(own_ref.dtype)
+    own_ref[2] = up.astype(own_ref.dtype)
 
     number = iter(range(copies))
 
@@ -152,6 +236,18 @@
     local.start()
     local_plan = pltpu.make_async_copy(plan_ref.at[me], plans_ref.at[me], lsem.at[1])
     local_plan.start()
+
+    center = wide[...]
+    above, below, left, right = around(center)
+    lap = above + below + left + right - 4.0 * center
+    row = lax.broadcasted_iota(jnp.int32, (center.shape[0], 1), 0)
+    col = lax.broadcasted_iota(jnp.int32, (1, center.shape[1]), 1)
+    row_keep = ((row >= 8) | (me > 0)) & ((row < 8 + tile_rows) | (me < n - 1))
+    col_keep = ((col >= 128) | (across > 0)) & ((col < 128 + tile_cols) | (across < n_dx - 1))
+    lap = jnp.where(row_keep & col_keep, lap, 0.0)
+    above, below, left, right = around(lap)
+    smooth_ref[...] = SMOOTHING_WEIGHT * inner(above + below + left + right - 4.0 * lap)
+
     mask_lists = [all_masks(order)[1:] for order in orders]
     for position in range(len(mask_lists[0])):
         for part, order in enumerate(orders):
@@ -167,32 +263,46 @@
         copy.wait_send()
     for copy in plan_copies:
         copy.wait()
+    for copy in halos:
+        copy.wait_send()
     local.wait()
     local_plan.wait()
 
 
-def gather_tiles(own, plan_by_dest, n):
-    bits = bit_count(n)
-    high = n // 2
-    copies = 2 * (high - 1) + 2 * high
+def gather_tiles(heights, albedo, plan_by_dest, n, n_dx):
+    copies = 2 * (n // 2 - 1) + n
+    tile_rows, tile_cols = heights.shape
+    vmem = pl.BlockSpec(memory_space=pltpu.VMEM)
+    hbm = pl.BlockSpec(memory_space=pl.ANY)
     return pl.pallas_call(
-        functools.partial(gather_kernel, n, copies),
+        functools.partial(gather_kernel, n, n_dx, copies),
         out_shape=(
-            jax.ShapeDtypeStruct((n,) + own.shape, own.dtype),
+            jax.ShapeDtypeStruct((n, 3, tile_rows, tile_cols), jnp.bfloat16),
             jax.ShapeDtypeStruct(plan_by_dest.shape, plan_by_dest.dtype),
+            jax.ShapeDtypeStruct(heights.shape, jnp.float32),
         ),
-        in_specs=[pl.BlockSpec(memory_space=pl.ANY)] * 2,
-        out_specs=(pl.BlockSpec(memory_space=pl.ANY),) * 2,
+        in_specs=[vmem, vmem, hbm],
+        out_specs=(hbm, hbm, vmem),
         scratch_shapes=[
+            pltpu.VMEM((3, tile_rows, tile_cols), jnp.bfloat16),
+            pltpu.VMEM((2, 8, tile_rows), jnp.float32),
+            pltpu.VMEM((2, 8, tile_cols), jnp.float32),
+            pltpu.VMEM((2, 8, tile_rows), jnp.float32),
+            pltpu.VMEM((4, 8, 128), jnp.float32),
+            pltpu.VMEM((tile_rows + 16, tile_cols + 256), jnp.float32),
             pltpu.SemaphoreType.DMA((copies,)),
             pltpu.SemaphoreType.DMA((copies,)),
             pltpu.SemaphoreType.DMA((n - 1,)),
             pltpu.SemaphoreType.DMA((n - 1,)),
+            pltpu.SemaphoreType.DMA((8,)),
+            pltpu.SemaphoreType.DMA((8,)),
             pltpu.SemaphoreType.DMA((2,)),
         ],
-        compiler_params=pltpu.CompilerParams(collective_id=0, has_side_effects=True),
+        compiler_params=pltpu.CompilerParams(
+            collective_id=0, has_side_effects=True, vmem_limit_bytes=VMEM_BYTES
+        ),
         name="gather_tiles",
-    )(own, plan_by_dest)
+    )(heights, albedo, plan_by_dest)
 
 
 def render_kernel(
@@ -302,17 +412,33 @@
 
 
 def scatter_kernel(
-    n, grads_ref, sums_ref, out_ref, camera_ref, first, later, csums, send, recv, csend, crecv
+    n,
+    n_dx,
+    grads_ref,
+    sums_ref,
+    smooth_ref,
+    height_ref,
+    camera_ref,
+    kept,
+    first,
+    later,
+    out_ref,
+    csums,
+    edges,
+    rims,
+    send,
+    recv,
+    csend,
+    crecv,
+    hsend,
+    hrecv,
+    lsem,
 ):
     bits = bit_count(n)
-    me = lax.axis_index("dy")
-    half = out_ref.shape[1] // 2
-    barrier = pltpu.get_barrier_semaphore()
-    for step in range(1, n):
-        pl.semaphore_signal(
-            barrier, inc=1, device_id={"dy": lax.rem(me + step, n)}, device_id_type=MESH
-        )
-    pl.semaphore_wait(barrier, n - 1)
+    me, across = lax.axis_index("dy"), lax.axis_index("dx")
+    tile_rows, tile_cols = height_ref.shape
+    half = tile_rows // 2
+    greet(n, n_dx, False)
 
     number = iter(range(send.shape[0]))
     started = []
@@ -335,6 +461,12 @@
     pair = {}
     for mask in masks:
         pair[mask] = push(grads_ref.at[flipped(me, mask + 1, bits)], first.at[mask >> 1], 0)
+    loads = {}
+    for mask in masks:
+        loads[mask] = pltpu.make_async_copy(
+            grads_ref.at[flipped(me, mask, bits)], kept.at[mask >> 1], lsem.at[mask >> 1]
+        )
+        loads[mask].start()
     camera_copies = []
     for step in range(1, n):
         to = lax.rem(me + step, n)
@@ -357,8 +489,9 @@
         return pl.ds(part * half, half)
 
     for mask in masks:
+        loads[mask].wait()
         pair[mask].wait_recv()
-        mine = grads_ref[flipped(me, mask, bits)].astype(jnp.float32)
+        mine = kept[mask >> 1].astype(jnp.float32)
         both = mine + first[mask >> 1].astype(jnp.float32)
         if mask == 0:
             out_ref[...] = both
@@ -387,6 +520,29 @@
                         source = first.at[mask >> 1, :, rows(part), :]
                         sent = push(source, later.at[to], bit)
                         coming[(part, mask ^ 1 << bit)] = (sent, to)
+    grad_x, grad_y = out_ref[0], out_ref[1]
+    edges[0] = columns_as_rows(grad_x, True)
+    edges[1] = columns_as_rows(grad_x, False)
+    edges[2] = grad_y[:8]
+    edges[3] = grad_y[tile_rows - 8 :]
+    targets = (
+        {"dx": lax.rem(across + n_dx - 1, n_dx)},
+        {"dx": lax.rem(across + 1, n_dx)},
+        {"dy": lax.rem(me + n - 1, n)},
+        {"dy": lax.rem(me + 1, n)},
+    )
+    halos = []
+    for c, device in enumerate(targets):
+        copy = pltpu.make_async_remote_copy(
+            src_ref=edges.at[c],
+            dst_ref=rims.at[c],
+            send_sem=hsend.at[c],
+            recv_sem=hrecv.at[c],
+            device_id=device,
+            device_id_type=MESH,
+        )
+        copy.start()
+        halos.append(copy)
     camera = sums_ref[me]
     for step in range(1, n):
         camera_copies[step - 1].wait()
@@ -394,42 +550,64 @@
     camera_ref[...] = camera
     for copy in started:
         copy.wait_send()
-
-
-def scatter_sums(grads, sums, n):
+    for copy in halos:
+        copy.wait()
+
+    after_x = jnp.where(across < n_dx - 1, rows_as_columns(rims[0], False), 0.0)[:, 0:1]
+    before_x = jnp.where(across > 0, rows_as_columns(rims[1], True), 0.0)[:, 127:128]
+    after_y = jnp.where(me < n - 1, rims[2], 0.0)[0:1]
+    before_y = jnp.where(me > 0, rims[3], 0.0)[7:8]
+    row = lax.broadcasted_iota(jnp.int32, (tile_rows, 1), 0)
+    col = lax.broadcasted_iota(jnp.int32, (1, tile_cols), 1)
+    left = jnp.where(col == 0, before_x, pltpu.roll(grad_x, 1, 1))
+    right = jnp.where(col == tile_cols - 1, after_x, pltpu.roll(grad_x, tile_cols - 1, 1))
+    above = jnp.where(row == 0, before_y, pltpu.roll(grad_y, 1, 0))
+    below = jnp.where(row == tile_rows - 1, after_y, pltpu.roll(grad_y, tile_rows - 1, 0))
+    height_ref[...] = 0.5 * ((left - right) + (above - below)) + smooth_ref[...]
+
+
+def scatter_sums(grads, sums, smooth, n, n_dx):
     _, parts, tile_rows, tile_cols = grads.shape
+    assert tile_rows == tile_cols
     high = n // 2
     halves = 2 * (high - 1)
     copies = high + halves
+    vmem = pl.BlockSpec(memory_space=pltpu.VMEM)
     return pl.pallas_call(
-        functools.partial(scatter_kernel, n),
+        functools.partial(scatter_kernel, n, n_dx),
         out_shape=(
-            jax.ShapeDtypeStruct(grads.shape[1:], jnp.float32),
+            jax.ShapeDtypeStruct(smooth.shape, jnp.float32),
             jax.ShapeDtypeStruct(sums.shape[1:], jnp.float32),
         ),
-        in_specs=[pl.BlockSpec(memory_space=pltpu.VMEM)] * 2,
-        out_specs=(pl.BlockSpec(memory_space=pltpu.VMEM),) * 2,
+        in_specs=[pl.BlockSpec(memory_space=pl.ANY), vmem, vmem],
+        out_specs=(vmem, vmem),
         scratch_shapes=[
             pltpu.VMEM((high, parts, tile_rows, tile_cols), grads.dtype),
+            pltpu.VMEM((high, parts, tile_rows, tile_cols), grads.dtype),
             pltpu.VMEM((halves, parts, tile_rows // 2, tile_cols), grads.dtype),
+            pltpu.VMEM((parts, tile_rows, tile_cols), jnp.float32),
             pltpu.VMEM((n - 1,) + sums.shape[1:], jnp.float32),
+            pltpu.VMEM((4, 8, tile_cols), jnp.float32),
+            pltpu.VMEM((4, 8, tile_cols), jnp.float32),
             pltpu.SemaphoreType.DMA((copies,)),
             pltpu.SemaphoreType.DMA((copies,)),
             pltpu.SemaphoreType.DMA((n - 1,)),
             pltpu.SemaphoreType.DMA((n - 1,)),
+            pltpu.SemaphoreType.DMA((4,)),
+            pltpu.SemaphoreType.DMA((4,)),
+            pltpu.SemaphoreType.DMA((high,)),
         ],
         compiler_params=pltpu.CompilerParams(
             collective_id=1, has_side_effects=True, vmem_limit_bytes=VMEM_BYTES
         ),
         name="scatter_sums",
-    )(grads, sums)
+    )(grads, sums, smooth)
 
 
 def per_device(
     heights, albedo, observed, resample, exposure, sun_azimuth, sun_elevation, send_plan, recv_plan
 ):
-    n = lax.axis_size("dy")
-    tile_rows, tile_cols = heights.shape
+    n, n_dx = lax.axis_size("dy"), lax.axis_size("dx")
     crops, size = observed.shape[0], observed.shape[-1]
     slot_count = send_plan.shape[-1]
     most = slot_count // n
@@ -445,27 +623,11 @@
         ((0, 0), (0, 6), (0, 128 - most)),
     )
 
-    wide_rim = padded_2(heights, (("dy", 0), ("dx", 1)), 2)
-    slope_x, slope_y = slopes(wide_rim[1:-1, 1:-1])
-    fields = shading(slope_x, slope_y, albedo).astype(jnp.bfloat16)
-    tiles, plans = gather_tiles(fields, plan_by_dest, n)
-
-    lap_field = laplace(wide_rim)
-    row_ids = jnp.arange(tile_rows + 2)
-    col_ids = jnp.arange(tile_cols + 2)
-    row_keep = ~(
-        (row_ids == 0) & (lax.axis_index("dy") == 0)
-        | (row_ids == tile_rows + 1) & (lax.axis_index("dy") == lax.axis_size("dy") - 1)
-    )
-    col_keep = ~(
-        (col_ids == 0) & (lax.axis_index("dx") == 0)
-        | (col_ids == tile_cols + 1) & (lax.axis_index("dx") == lax.axis_size("dx") - 1)
-    )
-    keep_mask = row_keep[:, None] & col_keep[None, :]
-    smoothness_term = laplace(jnp.where(keep_mask, lap_field, 0.0))
-
+    tiles, plans, smooth = gather_tiles(heights, albedo, plan_by_dest, n, n_dx)
     tile_grads, sums = render(plans, pick, used, light, tiles, resample, observed, most)
-    grads, camera = scatter_sums(tile_grads, sums.reshape(n, crops // n, 8, size), n)
+    height_gradient, camera = scatter_sums(
+        tile_grads, sums.reshape(n, crops // n, 8, size), smooth, n, n_dx
+    )
 
     coordinate = (jnp.arange(size, dtype=jnp.float32) - 0.5 * (size - 1)) / size
     plain = jnp.sum(camera, axis=-1)
@@ -483,13 +645,6 @@
         axis=-1,
     )
 
-    grad_x, grad_y = grads[0], grads[1]
-    low_x, high_x = shifted(grad_x.astype(jnp.bfloat16), "dx", 1, 1)
-    low_y, high_y = shifted(grad_y.astype(jnp.bfloat16), "dy", 0, 1)
-    rim_x = jnp.concatenate([low_x.astype(jnp.float32), grad_x, high_x.astype(jnp.float32)], axis=1)
-    rim_y = jnp.concatenate([low_y.astype(jnp.float32), grad_y, high_y.astype(jnp.float32)], axis=0)
-    data_term_gradient = (rim_x[:, :-2] - rim_x[:, 2:]) * 0.5 + (rim_y[:-2] - rim_y[2:]) * 0.5
-    height_gradient = data_term_gradient + SMOOTHING_WEIGHT * smoothness_term
     return (height_gradient, camera_model[None])
 
 

time: 205 us -> 180 us (0.88)
  starting transfers between devices: 21.3 us -> 0 us
  Pallas kernels: 154 us -> 169 us
  other arithmetic: 15.1 us -> 4.81 us
  waiting for transfers between devices: 5.15 us -> 0 us
  local copies, waits for them, and re-layouts: 8.29 us -> 5.67 us
    ppermute x8 -> x0, starting transfers between devices: 21.3 us -> none  [the longest x4 16.2 us: shifted(): lax.ppermute(lax.slice_in_dim(block, block.shape[dim] - width, None, axis...]
    pallas_call x2, Pallas kernels: 108 us -> 124 us  [the longest x1 71.2 us: gather_tiles(): pl.pallas_call(functools.partial(gather_kernel, n, n_dx, copies), out_sha...]
    ppermute x8 -> x0, waiting for transfers between devices: 5.15 us -> none  [the longest x4 3.46 us: shifted(): lax.ppermute(lax.slice_in_dim(block, 0, width, axis=dim), axis, backward)]
    add x1 -> x0, other arithmetic: 4.93 us -> none  [per_device(): height_gradient = data_term_gradient + SMOOTHING_WEIGHT * smoothness_term]
    another operation x3 -> x0, other arithmetic: 2.61 us -> none  [shading(): return jnp.stack([-slope_x * up, -slope_y * up, up])]
    concatenate x3 -> x0, other arithmetic: 2.18 us -> none  [padded_2(): block = jnp.concatenate([low, block, high], axis=dim)]
  transfers between devices with their start and end apart: 8 -> 0, of which waited for: 2 -> 0; matrix products, arithmetic and copies ran while one was open for 4% -> 0% of each run, Pallas kernels for 0% -> 0%
where the time goes in v1:
time: 180 us
  Pallas kernels  169 us (94%)
  local copies, waits for them, and re-layouts  5.67 us (3%)
  other arithmetic  4.81 us (3%)
    pallas_call x1, Pallas kernels, gather_tiles(): pl.pallas_call(functools.partial(gather_kernel, n, n_dx, copies), out_sha...  71.2 us
    pallas_call x1, Pallas kernels, scatter_sums(): pl.pallas_call(functools.partial(scatter_kernel, n, n_dx), out_shape=(jax...  52.7 us
    pallas_call x1, Pallas kernels, render(): pl.pallas_call(inner, out_shape=(jax.ShapeDtypeStruct((n, 2, tile_rows, t...  44.7 us

profile of v1, /device:TPU:0, one launch (start us, length us, event | category | flops | bytes accessed | tf_op | source)
XLA Modules:
  0.0 179.7 jit_solution(8440895400241119993)
XLA Ops:
  0.6 0.7 fusion
  1.3 0.7 cosine_multiply_fusion
  2.0 0.7 exp.3
  2.7 0.6 pad_maximum_fusion.light
  3.3 0.7 slice.24
  4.0 0.1 reshape_squeeze.3
  4.1 0.6 pad.4.plan_ref
  4.7 71.2 %gather_tiles.1 = (bf16[8,3,512,512]{3,2,1,0:T(8,128)(2,1)}, s32[8,8,128]{2,1,0:T(8,128)}, f32[512,512]{1,0:T(8,128)}) custom-call(f32[512,512]{1,0:T(8,128)} %heights_ref.1, f32[512,512]{1,0:T(8,128)} %albedo_ref.1, s32[8,8,128]{2,1,0:T(8,128)} %pad.4.plan_ref), custom_call_target="tpu_custom_call" | custom-call | tf_op jit(solution)/shard_map/gather_tiles/pallas_call | solution.py:277
  75.9 1.3 select_reduce_fusion.1
  77.3 0.7 select_reduce_fusion
  78.0 0.5 compare_convert_fusion.used
  78.5 44.7 %render.1 = (bf16[8,2,512,512]{3,2,1,0:T(8,128)(2,1)}, f32[16,8,384]{2,1,0:T(8,128)}) custom-call(s32[8,8,128]{2,1,0:T(8,128)} %get-tuple-element.10.plans, s32[24]{0:T(128)} %get-tuple-element.11.pick, s32[24]{0:T(128)} %compare_convert_fusion.used, f32[4,16]{1,0:T(4,128)} %pad_maximum_fusion.light, bf16[8,3,512,512]{3,2,1,0:T(8,128)(2,1)} %get-tuple-element.12.refs_0_, ...), custom_call_target="tpu_custom_call" | custom-call | tf_op jit(solution)/shard_map/render/pallas_call | solution.py:386
  123.2 52.7 %scatter_sums.1 = (f32[512,512]{1,0:T(8,128)}, f32[2,8,384]{2,1,0:T(8,128)}) custom-call(bf16[8,2,512,512]{3,2,1,0:T(8,128)(2,1)} %get-tuple-element.13.grads_ref, f32[8,2,8,384]{3,2,1,0:T(8,128)} %bitcast.6, f32[512,512]{1,0:T(8,128)} %get-tuple-element.15.smooth_ref), custom_call_target="tpu_custom_call" | custom-call | tf_op jit(solution)/shard_map/scatter_sums/pallas_call | solution.py:576
  175.9 0.8 multiply_reduce_fusion
  176.7 0.1 slice_multiply_fusion
  176.8 0.7 stack.2
  177.4 2.3 %copy.17 = f32[512,512]{1,0:T(8,128)} copy(f32[512,512]{1,0:T(8,128)} %get-tuple-element.35) | data formatting | bytes 2097152
  (2 shorter events, 0.0 us)

commit v2 on v1

--- a/solution.py
+++ b/solution.py
@@ -10,6 +10,13 @@
 SMOOTHING_WEIGHT = 0.02
 MESH = pl.DeviceIdType.MESH
 VMEM_BYTES = 56 * 1024 * 1024
+HEIGHT_SCALE = 8191.0
+FIELD_SCALE = 21844.0
+RIM_ROWS = 16
+
+
+def fixed_point(values, scale):
+    return jnp.floor(values * scale + 0.5).astype(jnp.int32).astype(jnp.int16)
 
 
 def sun_vectors(solar_azimuth, elevation):
@@ -106,8 +113,9 @@
     bits = bit_count(n)
     me, across = lax.axis_index("dy"), lax.axis_index("dx")
     tile_rows, tile_cols = heights_ref.shape
-    half = tile_rows // 2
+    cut = tile_rows + RIM_ROWS
     heights = heights_ref[...]
+    own_ref[0:tile_rows] = fixed_point(heights, HEIGHT_SCALE)
     edges[0] = columns_as_rows(heights, True)
     edges[1] = columns_as_rows(heights, False)
     greet(n, n_dx, True)
@@ -174,26 +182,18 @@
             pltpu.roll(block, cols_all - 1, 1),
         )
 
-    above, below, left, right = around(wide[...])
-    slope_x = inner(right - left) * 0.5
-    slope_y = inner(below - above) * 0.5
-    up = albedo_ref[...] * lax.rsqrt(1.0 + slope_x * slope_x + slope_y * slope_y)
-    own_ref[0] = (-slope_x * up).astype(own_ref.dtype)
-    own_ref[1] = (-slope_y * up).astype(own_ref.dtype)
-    own_ref[2] = up.astype(own_ref.dtype)
-
     number = iter(range(copies))
 
     def rows(part):
-        return pl.ds(part * half, half)
+        return pl.ds(part * cut, tile_rows if part else cut)
 
     def make(mask, part, bit):
         tile = flipped(me, mask, bits)
         source = own_ref if mask == 0 else out_ref.at[tile]
         c = next(number)
         return pltpu.make_async_remote_copy(
-            src_ref=source.at[:, rows(part), :],
-            dst_ref=out_ref.at[tile, :, rows(part), :],
+            src_ref=source.at[rows(part), :],
+            dst_ref=out_ref.at[tile, rows(part), :],
             send_sem=send.at[c],
             recv_sem=recv.at[c],
             device_id={"dy": flipped(me, 1 << bit, bits)},
@@ -214,9 +214,22 @@
         seen = [k for k, bit in enumerate(order) if mask >> bit & 1]
         return order[(max(seen) + 1 if seen else 0) :]
 
+    place = lax.broadcasted_iota(jnp.int32, (RIM_ROWS, 1), 0)
+    rim = jnp.where(place == 0, jnp.where(across < n_dx - 1, col_rim[0], 0.0)[0:1], 0.0)
+    rim = jnp.where(place == 1, jnp.where(me < n - 1, row_rim[0], 0.0)[0:1], rim)
+    rim = jnp.where(place == RIM_ROWS - 2, jnp.where(me > 0, row_rim[1], 0.0)[7:8], rim)
+    rim = jnp.where(place == RIM_ROWS - 1, jnp.where(across > 0, col_rim[1], 0.0)[7:8], rim)
+    own_ref[pl.ds(tile_rows, RIM_ROWS)] = fixed_point(rim, HEIGHT_SCALE)
     for position in range(bits - 1):
-        for part, order in enumerate(orders):
-            forward(0, part, order[position])
+        forward(0, 0, orders[0][position])
+
+    above, below, left, right = around(wide[...])
+    slope_x = inner(right - left) * 0.5
+    slope_y = inner(below - above) * 0.5
+    up = albedo_ref[...] * lax.rsqrt(1.0 + slope_x * slope_x + slope_y * slope_y)
+    own_ref[pl.ds(cut, tile_rows)] = fixed_point(up, FIELD_SCALE)
+    for position in range(bits - 1):
+        forward(0, 1, orders[1][position])
     plan_copies = []
     for step in range(1, n):
         to = lax.rem(me + step, n)
@@ -277,14 +290,14 @@
     return pl.pallas_call(
         functools.partial(gather_kernel, n, n_dx, copies),
         out_shape=(
-            jax.ShapeDtypeStruct((n, 3, tile_rows, tile_cols), jnp.bfloat16),
+            jax.ShapeDtypeStruct((n, 2 * tile_rows + RIM_ROWS, tile_cols), jnp.int16),
             jax.ShapeDtypeStruct(plan_by_dest.shape, plan_by_dest.dtype),
             jax.ShapeDtypeStruct(heights.shape, jnp.float32),
         ),
         in_specs=[vmem, vmem, hbm],
         out_specs=(hbm, hbm, vmem),
         scratch_shapes=[
-            pltpu.VMEM((3, tile_rows, tile_cols), jnp.bfloat16),
+            pltpu.VMEM((2 * tile_rows + RIM_ROWS, tile_cols), jnp.int16),
             pltpu.VMEM((2, 8, tile_rows), jnp.float32),
             pltpu.VMEM((2, 8, tile_cols), jnp.float32),
             pltpu.VMEM((2, 8, tile_rows), jnp.float32),
@@ -306,7 +319,7 @@
 
 
 def render_kernel(
-    plans, pick, used, light, tiles_ref, mats_ref, seen_ref, grads_ref, sums_ref, total
+    plans, pick, used, light, tile_ref, mats_ref, seen_ref, grads_ref, sums_ref, total, fields
 ):
     tile, slot = pl.program_id(0), pl.program_id(1)
     most = pl.num_programs(1)
@@ -316,6 +329,28 @@
     @pl.when(slot == 0)
     def _():
         total[...] = jnp.zeros_like(total)
+        _, tile_rows, tile_cols = fields.shape
+        ahead = tile_rows + RIM_ROWS
+
+        def real(first, count):
+            return tile_ref[0, pl.ds(first, count)].astype(jnp.int32).astype(jnp.float32)
+
+        heights = real(0, tile_rows)
+        rim = real(tile_rows, RIM_ROWS)
+        side = RIM_ROWS // 2
+        gap = jnp.zeros((128 - RIM_ROWS, tile_cols), jnp.float32)
+        sides = jnp.transpose(jnp.concatenate([rim[:side], gap, rim[side:]], axis=0))
+        across = jnp.concatenate([heights, sides], axis=1)
+        right = pltpu.roll(across, tile_cols + 127, 1)[:, :tile_cols]
+        left = pltpu.roll(across, 1, 1)[:, :tile_cols]
+        line = lax.broadcasted_iota(jnp.int32, (tile_rows, 1), 0)
+        above = jnp.where(line == 0, rim[RIM_ROWS - 2 : RIM_ROWS - 1], pltpu.roll(heights, 1, 0))
+        below = jnp.where(line == tile_rows - 1, rim[1:2], pltpu.roll(heights, tile_rows - 1, 0))
+        up = real(ahead, tile_rows) * (1.0 / FIELD_SCALE)
+        slope_up = up * (0.5 / HEIGHT_SCALE)
+        fields[0] = (left - right) * slope_up
+        fields[1] = (above - below) * slope_up
+        fields[2] = up
 
     @pl.when(used[step] == 1)
     def _():
@@ -326,7 +361,7 @@
         gain = light[3, image]
 
         def field(k):
-            return tiles_ref[0, k, rows, cols].astype(jnp.float32)
+            return fields[k, rows, cols]
 
         shaded = (sun_x * field(0) + sun_y * field(1) + sun_z * field(2)).astype(jnp.bfloat16)
         first = jnp.dot(mats_ref[0, 0], shaded, preferred_element_type=jnp.float32)
@@ -351,19 +386,22 @@
         below = jnp.where(row == last, predicted, pltpu.roll(predicted, last, 0))
         above = jnp.where(row == 0, predicted, pltpu.roll(predicted, 1, 0))
         col_weight = jnp.where((col == 0) | (col == last), 1.0, 0.5)
-        row_weight = jnp.where((row == 0) | (row == last), 1.0, 0.5)
         row_place = (row.astype(jnp.float32) - 0.5 * (size - 1)) / size
         by_u = residual * (right - left)
-        by_v = residual * ((below - above) * row_weight)
+        by_v = residual * (below - above)
+        ends = 0.5 * (by_v[0:1] + by_v[last:])
+        tilt = 0.5 * (0.5 * (size - 1) / size) * (by_v[last:] - by_v[0:1])
         sums_ref[image, 0:1] = col_weight * jnp.sum(by_u, axis=0, keepdims=True)
         sums_ref[image, 1:2] = col_weight * jnp.sum(by_u * row_place, axis=0, keepdims=True)
-        sums_ref[image, 2:3] = jnp.sum(by_v, axis=0, keepdims=True)
-        sums_ref[image, 3:4] = jnp.sum(by_v * row_place, axis=0, keepdims=True)
+        sums_ref[image, 2:3] = 0.5 * jnp.sum(by_v, axis=0, keepdims=True) + ends
+        sums_ref[image, 3:4] = 0.5 * jnp.sum(by_v * row_place, axis=0, keepdims=True) + tilt
         sums_ref[image, 4:5] = jnp.sum(residual * predicted, axis=0, keepdims=True)
         sums_ref[image, 5:8] = jnp.zeros((3, size), jnp.float32)
 
         fx, fy, fz = field(0), field(1), field(2)
-        along = (sun_x * fx + sun_y * fy + sun_z * fz) / (fx * fx + fy * fy + fz * fz)
+        along = (sun_x * fx + sun_y * fy + sun_z * fz) * pl.reciprocal(
+            fx * fx + fy * fy + fz * fz, approx=True
+        )
         scaled = crop_grad * fz
         total[0, rows, cols] += scaled * (fx * along - sun_x)
         total[1, rows, cols] += scaled * (fy * along - sun_y)
@@ -374,7 +412,8 @@
 
 
 def render(plans, pick, used, light, tiles, resample, observed, most):
-    n, _, tile_rows, tile_cols = tiles.shape
+    n, packed_rows, tile_cols = tiles.shape
+    tile_rows = (packed_rows - RIM_ROWS) // 2
     crops, size, _ = observed.shape
 
     def crop_at(t, j, plans, pick, used):
@@ -394,7 +433,7 @@
             grid=(n, most),
             in_specs=[
                 pl.BlockSpec(memory_space=pltpu.SMEM),
-                pl.BlockSpec((1, 3, tile_rows, tile_cols), lambda t, j, *s: (t, 0, 0, 0)),
+                pl.BlockSpec((1, packed_rows, tile_cols), lambda t, j, *s: (t, 0, 0)),
                 pl.BlockSpec((1, 2, size, size), lambda t, j, *s: (crop_at(t, j, *s), 0, 0, 0)),
                 pl.BlockSpec((1, size, size), lambda t, j, *s: (crop_at(t, j, *s), 0, 0)),
             ],
@@ -402,7 +441,10 @@
                 pl.BlockSpec((1, 2, tile_rows, tile_cols), lambda t, j, *s: (t, 0, 0, 0)),
                 pl.BlockSpec((crops, 8, size), lambda t, j, *s: (0, 0, 0)),
             ),
-            scratch_shapes=[pltpu.VMEM((2, tile_rows, tile_cols), jnp.float32)],
+            scratch_shapes=[
+                pltpu.VMEM((2, tile_rows, tile_cols), jnp.float32),
+                pltpu.VMEM((3, tile_rows, tile_cols), jnp.float32),
+            ],
         ),
         compiler_params=pltpu.CompilerParams(
             dimension_semantics=("arbitrary", "arbitrary"), vmem_limit_bytes=VMEM_BYTES
@@ -459,8 +501,11 @@
 
     masks = [m << 1 for m in range(n // 2)][::-1]
     pair = {}
-    for mask in masks:
+
+    def push_pair(mask):
         pair[mask] = push(grads_ref.at[flipped(me, mask + 1, bits)], first.at[mask >> 1], 0)
+
+    push_pair(masks[0])
     loads = {}
     for mask in masks:
         loads[mask] = pltpu.make_async_copy(
@@ -491,6 +536,8 @@
     for mask in masks:
         loads[mask].wait()
         pair[mask].wait_recv()
+        if mask:
+            push_pair(mask - 2)
         mine = kept[mask >> 1].astype(jnp.float32)
         both = mine + first[mask >> 1].astype(jnp.float32)
         if mask == 0:

time: 180 us -> 166 us (0.922)
  Pallas kernels: 169 us -> 155 us
    pallas_call x1, Pallas kernels: 71.2 us -> 53.9 us  [gather_tiles(): pl.pallas_call(functools.partial(gather_kernel, n, n_dx, copies), out_sha...]
    pallas_call x1, Pallas kernels: 44.7 us -> 48.8 us  [render(): pl.pallas_call(inner, out_shape=(jax.ShapeDtypeStruct((n, 2, tile_rows, t...]
where the time goes in v2:
time: 166 us
  Pallas kernels  155 us (93%)
  local copies, waits for them, and re-layouts  5.67 us (3%)
  other arithmetic  4.8 us (3%)
    pallas_call x1, Pallas kernels, gather_tiles(): pl.pallas_call(functools.partial(gather_kernel, n, n_dx, copies), out_sha...  53.9 us
    pallas_call x1, Pallas kernels, scatter_sums(): pl.pallas_call(functools.partial(scatter_kernel, n, n_dx), out_shape=(jax...  52.2 us
    pallas_call x1, Pallas kernels, render(): pl.pallas_call(inner, out_shape=(jax.ShapeDtypeStruct((n, 2, tile_rows, t...  48.8 us

profile of v2, /device:TPU:0, one launch (start us, length us, event | category | flops | bytes accessed | tf_op | source)
XLA Modules:
  0.0 166.0 jit_solution(7148447029700619732)
XLA Ops:
  0.6 0.7 fusion
  1.3 0.7 cosine_multiply_fusion
  2.0 0.7 exp.3
  2.7 0.6 pad_maximum_fusion.light
  3.3 0.7 slice.24
  4.0 0.1 reshape_squeeze.3
  4.1 0.6 pad.4.plan_ref
  4.7 53.9 %gather_tiles.1 = (s16[8,1040,512]{2,1,0:T(8,128)(2,1)}, s32[8,8,128]{2,1,0:T(8,128)}, f32[512,512]{1,0:T(8,128)}) custom-call(f32[512,512]{1,0:T(8,128)} %heights_ref.1, f32[512,512]{1,0:T(8,128)} %albedo_ref.1, s32[8,8,128]{2,1,0:T(8,128)} %pad.4.plan_ref), custom_call_target="tpu_custom_call" | custom-call | tf_op jit(solution)/shard_map/gather_tiles/pallas_call | solution.py:290
  58.6 1.3 select_reduce_fusion.1
  59.9 0.7 select_reduce_fusion
  60.7 0.5 compare_convert_fusion.used
  61.2 48.8 %render.1 = (bf16[8,2,512,512]{3,2,1,0:T(8,128)(2,1)}, f32[16,8,384]{2,1,0:T(8,128)}) custom-call(s32[8,8,128]{2,1,0:T(8,128)} %get-tuple-element.10.plans, s32[24]{0:T(128)} %get-tuple-element.11.pick, s32[24]{0:T(128)} %compare_convert_fusion.used, f32[4,16]{1,0:T(4,128)} %pad_maximum_fusion.light, s16[8,1040,512]{2,1,0:T(8,128)(2,1)} %get-tuple-element.12.refs_0_, ...), custom_call_target="tpu_custom_call" | custom-call | tf_op jit(solution)/shard_map/render/pallas_call | solution.py:425
  110.0 52.2 %scatter_sums.1 = (f32[512,512]{1,0:T(8,128)}, f32[2,8,384]{2,1,0:T(8,128)}) custom-call(bf16[8,2,512,512]{3,2,1,0:T(8,128)(2,1)} %get-tuple-element.13.grads_ref, f32[8,2,8,384]{3,2,1,0:T(8,128)} %bitcast.6, f32[512,512]{1,0:T(8,128)} %get-tuple-element.15.smooth_ref), custom_call_target="tpu_custom_call" | custom-call | tf_op jit(solution)/shard_map/scatter_sums/pallas_call | solution.py:623
  162.2 0.8 multiply_reduce_fusion
  163.0 0.1 slice_multiply_fusion
  163.1 0.7 stack.2
  163.8 2.3 %copy.17 = f32[512,512]{1,0:T(8,128)} copy(f32[512,512]{1,0:T(8,128)} %get-tuple-element.35) | data formatting | bytes 2097152
  (2 shorter events, 0.0 us)

commit v3 on v2

--- a/solution.py
+++ b/solution.py
@@ -408,7 +408,22 @@
 
     @pl.when(slot == most - 1)
     def _():
-        grads_ref[0] = total[...].astype(grads_ref.dtype)
+        _, tile_rows, tile_cols = total.shape
+        grad_x, grad_y = 0.5 * total[0], 0.5 * total[1]
+        line = lax.broadcasted_iota(jnp.int32, (tile_rows, 1), 0)
+        place = lax.broadcasted_iota(jnp.int32, (1, tile_cols), 1)
+        left = jnp.where(place == 0, 0.0, pltpu.roll(grad_x, 1, 1))
+        right = jnp.where(place == tile_cols - 1, 0.0, pltpu.roll(grad_x, tile_cols - 1, 1))
+        above = jnp.where(line == 0, 0.0, pltpu.roll(grad_y, 1, 0))
+        below = jnp.where(line == tile_rows - 1, 0.0, pltpu.roll(grad_y, tile_rows - 1, 0))
+        spread = (left - right) + (above - below)
+        grads_ref[0, 0:tile_rows] = spread.astype(grads_ref.dtype)
+        at = lax.broadcasted_iota(jnp.int32, (RIM_ROWS, 1), 0)
+        rim = jnp.where(at == 0, grad_y[0:1], 0.0)
+        rim = jnp.where(at == 1, grad_y[tile_rows - 1 :], rim)
+        rim = jnp.where(at == 2, columns_as_rows(grad_x, True)[0:1], rim)
+        rim = jnp.where(at == 3, columns_as_rows(grad_x, False)[7:8], rim)
+        grads_ref[0, pl.ds(tile_rows, RIM_ROWS)] = rim.astype(grads_ref.dtype)
 
 
 def render(plans, pick, used, light, tiles, resample, observed, most):
@@ -425,7 +440,7 @@
     return pl.pallas_call(
         inner,
         out_shape=(
-            jax.ShapeDtypeStruct((n, 2, tile_rows, tile_cols), jnp.bfloat16),
+            jax.ShapeDtypeStruct((n, tile_rows + RIM_ROWS, tile_cols), jnp.bfloat16),
             jax.ShapeDtypeStruct((crops, 8, size), jnp.float32),
         ),
         grid_spec=pltpu.PrefetchScalarGridSpec(
@@ -438,7 +453,7 @@
                 pl.BlockSpec((1, size, size), lambda t, j, *s: (crop_at(t, j, *s), 0, 0)),
             ],
             out_specs=(
-                pl.BlockSpec((1, 2, tile_rows, tile_cols), lambda t, j, *s: (t, 0, 0, 0)),
+                pl.BlockSpec((1, tile_rows + RIM_ROWS, tile_cols), lambda t, j, *s: (t, 0, 0)),
                 pl.BlockSpec((crops, 8, size), lambda t, j, *s: (0, 0, 0)),
             ),
             scratch_shapes=[
@@ -466,7 +481,6 @@
     later,
     out_ref,
     csums,
-    edges,
     rims,
     send,
     recv,
@@ -531,7 +545,10 @@
     coming = {}
 
     def rows(part):
-        return pl.ds(part * half, half)
+        return pl.ds(part * half, half + part * RIM_ROWS)
+
+    def landing(at, part):
+        return later.at[at, pl.ds(0, half + part * RIM_ROWS), :]
 
     for mask in masks:
         loads[mask].wait()
@@ -547,31 +564,27 @@
             for part, order in enumerate(orders):
                 if mask >> order[0] & 1:
                     at = next(places)
-                    source = first.at[mask >> 1, :, rows(part), :]
-                    copy = push(source, later.at[at], order[0])
+                    source = first.at[mask >> 1, rows(part), :]
+                    copy = push(source, landing(at, part), order[0])
                     coming[(part, mask ^ 1 << order[0])] = (copy, at)
     for stage in range(bits - 1):
-        for part, order in enumerate(orders):
-            landed = [(m, coming.pop((p, m))) for p, m in list(coming) if p == part]
-            for mask, (copy, at) in landed:
-                copy.wait_recv()
-                add = later[at].astype(jnp.float32)
-                if mask == 0:
-                    out_ref[:, rows(part), :] += add
-                else:
-                    held = first[mask >> 1, :, rows(part), :].astype(jnp.float32)
-                    first[mask >> 1, :, rows(part), :] = (held + add).astype(first.dtype)
-                    bit = order[stage + 1]
-                    if mask >> bit & 1:
-                        to = next(places)
-                        source = first.at[mask >> 1, :, rows(part), :]
-                        sent = push(source, later.at[to], bit)
-                        coming[(part, mask ^ 1 << bit)] = (sent, to)
-    grad_x, grad_y = out_ref[0], out_ref[1]
-    edges[0] = columns_as_rows(grad_x, True)
-    edges[1] = columns_as_rows(grad_x, False)
-    edges[2] = grad_y[:8]
-    edges[3] = grad_y[tile_rows - 8 :]
+        landed = sorted(coming.items(), key=lambda item: item[0][1] == 0)
+        coming = {}
+        for (part, mask), (copy, at) in landed:
+            order = orders[part]
+            copy.wait_recv()
+            add = landing(at, part)[...].astype(jnp.float32)
+            if mask == 0:
+                out_ref[rows(part), :] += add
+            else:
+                held = first[mask >> 1, rows(part), :].astype(jnp.float32)
+                first[mask >> 1, rows(part), :] = (held + add).astype(first.dtype)
+                bit = order[stage + 1]
+                if mask >> bit & 1:
+                    to = next(places)
+                    source = first.at[mask >> 1, rows(part), :]
+                    sent = push(source, landing(to, part), bit)
+                    coming[(part, mask ^ 1 << bit)] = (sent, to)
     targets = (
         {"dx": lax.rem(across + n_dx - 1, n_dx)},
         {"dx": lax.rem(across + 1, n_dx)},
@@ -581,7 +594,7 @@
     halos = []
     for c, device in enumerate(targets):
         copy = pltpu.make_async_remote_copy(
-            src_ref=edges.at[c],
+            src_ref=out_ref.at[pl.ds(tile_rows, 8)],
             dst_ref=rims.at[c],
             send_sem=hsend.at[c],
             recv_sem=hrecv.at[c],
@@ -600,21 +613,24 @@
     for copy in halos:
         copy.wait()
 
-    after_x = jnp.where(across < n_dx - 1, rows_as_columns(rims[0], False), 0.0)[:, 0:1]
-    before_x = jnp.where(across > 0, rows_as_columns(rims[1], True), 0.0)[:, 127:128]
+    after_x = jnp.where(across < n_dx - 1, rims[0], 0.0)
+    before_x = jnp.where(across > 0, rims[1], 0.0)
     after_y = jnp.where(me < n - 1, rims[2], 0.0)[0:1]
-    before_y = jnp.where(me > 0, rims[3], 0.0)[7:8]
+    before_y = jnp.where(me > 0, rims[3], 0.0)[1:2]
+    gap = jnp.zeros((112, tile_rows), jnp.float32)
+    sides = jnp.transpose(jnp.concatenate([after_x, before_x, gap], axis=0))
     row = lax.broadcasted_iota(jnp.int32, (tile_rows, 1), 0)
     col = lax.broadcasted_iota(jnp.int32, (1, tile_cols), 1)
-    left = jnp.where(col == 0, before_x, pltpu.roll(grad_x, 1, 1))
-    right = jnp.where(col == tile_cols - 1, after_x, pltpu.roll(grad_x, tile_cols - 1, 1))
-    above = jnp.where(row == 0, before_y, pltpu.roll(grad_y, 1, 0))
-    below = jnp.where(row == tile_rows - 1, after_y, pltpu.roll(grad_y, tile_rows - 1, 0))
-    height_ref[...] = 0.5 * ((left - right) + (above - below)) + smooth_ref[...]
+    rim = jnp.where(col == tile_cols - 1, -sides[:, 2:3], 0.0)
+    rim = rim + jnp.where(col == 0, sides[:, 11:12], 0.0)
+    rim = rim + jnp.where(row == tile_rows - 1, -after_y, 0.0)
+    rim = rim + jnp.where(row == 0, before_y, 0.0)
+    height_ref[...] = out_ref[0:tile_rows] + smooth_ref[...] + rim
 
 
 def scatter_sums(grads, sums, smooth, n, n_dx):
-    _, parts, tile_rows, tile_cols = grads.shape
+    _, sent_rows, tile_cols = grads.shape
+    tile_rows = smooth.shape[0]
     assert tile_rows == tile_cols
     high = n // 2
     halves = 2 * (high - 1)
@@ -629,12 +645,11 @@
         in_specs=[pl.BlockSpec(memory_space=pl.ANY), vmem, vmem],
         out_specs=(vmem, vmem),
         scratch_shapes=[
-            pltpu.VMEM((high, parts, tile_rows, tile_cols), grads.dtype),
-            pltpu.VMEM((high, parts, tile_rows, tile_cols), grads.dtype),
-            pltpu.VMEM((halves, parts, tile_rows // 2, tile_cols), grads.dtype),
-            pltpu.VMEM((parts, tile_rows, tile_cols), jnp.float32),
+            pltpu.VMEM((high, sent_rows, tile_cols), grads.dtype),
+            pltpu.VMEM((high, sent_rows, tile_cols), grads.dtype),
+            pltpu.VMEM((halves, sent_rows - tile_rows // 2, tile_cols), grads.dtype),
+            pltpu.VMEM((sent_rows, tile_cols), jnp.float32),
             pltpu.VMEM((n - 1,) + sums.shape[1:], jnp.float32),
-            pltpu.VMEM((4, 8, tile_cols), jnp.float32),
             pltpu.VMEM((4, 8, tile_cols), jnp.float32),
             pltpu.SemaphoreType.DMA((copies,)),
             pltpu.SemaphoreType.DMA((copies,)),

time: 166 us -> 150 us (0.904)
  Pallas kernels: 155 us -> 138 us
    pallas_call x1, Pallas kernels: 52.2 us -> 31 us  [scatter_sums(): pl.pallas_call(functools.partial(scatter_kernel, n, n_dx), out_shape=(jax...]
    pallas_call x1, Pallas kernels: 48.8 us -> 53 us  [render(): pl.pallas_call(inner, out_shape=(jax.ShapeDtypeStruct((n, tile_rows + RIM...]
where the time goes in v3:
time: 150 us; the launch traced here: 149 us
  Pallas kernels  138 us (92%)
  local copies, waits for them, and re-layouts  5.67 us (4%)
  other arithmetic  4.82 us (3%)
    pallas_call x1, Pallas kernels, gather_tiles(): pl.pallas_call(functools.partial(gather_kernel, n, n_dx, copies), out_sha...  54 us
    pallas_call x1, Pallas kernels, render(): pl.pallas_call(inner, out_shape=(jax.ShapeDtypeStruct((n, tile_rows + RIM...  53 us
    pallas_call x1, Pallas kernels, scatter_sums(): pl.pallas_call(functools.partial(scatter_kernel, n, n_dx), out_shape=(jax...  31 us

profile of v3, /device:TPU:0, one launch (start us, length us, event | category | flops | bytes accessed | tf_op | source)
XLA Modules:
  0.0 149.1 jit_solution(14719919114756225276)
XLA Ops:
  0.6 0.7 fusion
  1.3 0.7 cosine_multiply_fusion
  2.0 0.7 exp.3
  2.7 0.6 pad_maximum_fusion.light
  3.3 0.7 slice.24
  4.0 0.1 reshape_squeeze.3
  4.1 0.6 pad.4.plan_ref
  4.7 54.0 %gather_tiles.1 = (s16[8,1040,512]{2,1,0:T(8,128)(2,1)}, s32[8,8,128]{2,1,0:T(8,128)}, f32[512,512]{1,0:T(8,128)}) custom-call(f32[512,512]{1,0:T(8,128)} %heights_ref.1, f32[512,512]{1,0:T(8,128)} %albedo_ref.1, s32[8,8,128]{2,1,0:T(8,128)} %pad.4.plan_ref), custom_call_target="tpu_custom_call" | custom-call | tf_op jit(solution)/shard_map/gather_tiles/pallas_call | solution.py:290
  58.7 1.3 select_reduce_fusion.1
  60.1 0.7 select_reduce_fusion
  60.8 0.5 compare_convert_fusion.used
  61.3 53.0 %render.1 = (bf16[8,528,512]{2,1,0:T(8,128)(2,1)}, f32[16,8,384]{2,1,0:T(8,128)}) custom-call(s32[8,8,128]{2,1,0:T(8,128)} %get-tuple-element.10.plans, s32[24]{0:T(128)} %get-tuple-element.11.pick, s32[24]{0:T(128)} %compare_convert_fusion.used, f32[4,16]{1,0:T(4,128)} %pad_maximum_fusion.light, s16[8,1040,512]{2,1,0:T(8,128)(2,1)} %get-tuple-element.12.refs_0_, ...), custom_call_target="tpu_custom_call" | custom-call | tf_op jit(solution)/shard_map/render/pallas_call | solution.py:440
  114.3 31.0 %scatter_sums.1 = (f32[512,512]{1,0:T(8,128)}, f32[2,8,384]{2,1,0:T(8,128)}) custom-call(bf16[8,528,512]{2,1,0:T(8,128)(2,1)} %get-tuple-element.13.grads_ref, f32[8,2,8,384]{3,2,1,0:T(8,128)} %bitcast.6, f32[512,512]{1,0:T(8,128)} %get-tuple-element.15.smooth_ref), custom_call_target="tpu_custom_call" | custom-call | tf_op jit(solution)/shard_map/scatter_sums/pallas_call | solution.py:639
  145.3 0.8 multiply_reduce_fusion
  146.1 0.1 slice_multiply_fusion
  146.2 0.7 stack.2
  146.9 2.3 %copy.17 = f32[512,512]{1,0:T(8,128)} copy(f32[512,512]{1,0:T(8,128)} %get-tuple-element.35) | data formatting | bytes 2097152
  (2 shorter events, 0.0 us)

commit v4 on v3

--- a/solution.py
+++ b/solution.py
@@ -150,6 +150,40 @@
                 corner_rim.at[up * 2 + right],
                 {"dy": row_to[up], "dx": col_to[right]},
             )
+    number = iter(range(copies))
+
+    def rows(part):
+        return pl.ds(part * tile_rows, cut if part else tile_rows)
+
+    def make(mask, part, bit):
+        tile = flipped(me, mask, bits)
+        source = own_ref if mask == 0 else out_ref.at[tile]
+        c = next(number)
+        return pltpu.make_async_remote_copy(
+            src_ref=source.at[rows(part), :],
+            dst_ref=out_ref.at[tile, rows(part), :],
+            send_sem=send.at[c],
+            recv_sem=recv.at[c],
+            device_id={"dy": flipped(me, 1 << bit, bits)},
+            device_id_type=MESH,
+        )
+
+    orders = bit_orders(bits)
+    started = []
+    arriving = {}
+
+    def forward(mask, part, over):
+        copy = make(mask, part, over)
+        copy.start()
+        started.append(copy)
+        arriving[(mask | 1 << over, part)] = copy
+
+    def later(mask, order):
+        seen = [k for k, bit in enumerate(order) if mask >> bit & 1]
+        return order[(max(seen) + 1 if seen else 0) :]
+
+    for position in range(bits - 1):
+        forward(0, 0, orders[0][position])
     for copy in halos:
         copy.wait_recv()
 
@@ -182,46 +216,12 @@
             pltpu.roll(block, cols_all - 1, 1),
         )
 
-    number = iter(range(copies))
-
-    def rows(part):
-        return pl.ds(part * cut, tile_rows if part else cut)
-
-    def make(mask, part, bit):
-        tile = flipped(me, mask, bits)
-        source = own_ref if mask == 0 else out_ref.at[tile]
-        c = next(number)
-        return pltpu.make_async_remote_copy(
-            src_ref=source.at[rows(part), :],
-            dst_ref=out_ref.at[tile, rows(part), :],
-            send_sem=send.at[c],
-            recv_sem=recv.at[c],
-            device_id={"dy": flipped(me, 1 << bit, bits)},
-            device_id_type=MESH,
-        )
-
-    orders = bit_orders(bits)
-    started = []
-    arriving = {}
-
-    def forward(mask, part, over):
-        copy = make(mask, part, over)
-        copy.start()
-        started.append(copy)
-        arriving[(mask | 1 << over, part)] = copy
-
-    def later(mask, order):
-        seen = [k for k, bit in enumerate(order) if mask >> bit & 1]
-        return order[(max(seen) + 1 if seen else 0) :]
-
     place = lax.broadcasted_iota(jnp.int32, (RIM_ROWS, 1), 0)
     rim = jnp.where(place == 0, jnp.where(across < n_dx - 1, col_rim[0], 0.0)[0:1], 0.0)
     rim = jnp.where(place == 1, jnp.where(me < n - 1, row_rim[0], 0.0)[0:1], rim)
     rim = jnp.where(place == RIM_ROWS - 2, jnp.where(me > 0, row_rim[1], 0.0)[7:8], rim)
     rim = jnp.where(place == RIM_ROWS - 1, jnp.where(across > 0, col_rim[1], 0.0)[7:8], rim)
     own_ref[pl.ds(tile_rows, RIM_ROWS)] = fixed_point(rim, HEIGHT_SCALE)
-    for position in range(bits - 1):
-        forward(0, 0, orders[0][position])
 
     above, below, left, right = around(wide[...])
     slope_x = inner(right - left) * 0.5
@@ -319,7 +319,7 @@
 
 
 def render_kernel(
-    plans, pick, used, light, tile_ref, mats_ref, seen_ref, grads_ref, sums_ref, total, fields
+    plans, pick, light, tile_ref, mats_ref, seen_ref, grads_ref, sums_ref, total, fields
 ):
     tile, slot = pl.program_id(0), pl.program_id(1)
     most = pl.num_programs(1)
@@ -352,9 +352,11 @@
         fields[1] = (above - below) * slope_up
         fields[2] = up
 
-    @pl.when(used[step] == 1)
+    crops = sums_ref.shape[0]
+
+    @pl.when(pick[step] >= crops)
     def _():
-        image = pick[step]
+        image = pick[step] - crops
         rows = pl.ds(pl.multiple_of(plans[tile, 0, slot], 128), size)
         cols = pl.ds(pl.multiple_of(plans[tile, 1, slot], 128), size)
         sun_x, sun_y, sun_z = light[0, image], light[1, image], light[2, image]
@@ -426,25 +428,22 @@
         grads_ref[0, pl.ds(tile_rows, RIM_ROWS)] = rim.astype(grads_ref.dtype)
 
 
-def render(plans, pick, used, light, tiles, resample, observed, most):
+def render(plans, pick, light, tiles, resample, observed, most):
     n, packed_rows, tile_cols = tiles.shape
     tile_rows = (packed_rows - RIM_ROWS) // 2
     crops, size, _ = observed.shape
 
-    def crop_at(t, j, plans, pick, used):
-        return pick[t * most + j]
-
-    def inner(plans, pick, used, light, *refs):
-        render_kernel(plans, pick, used, light, *refs)
+    def crop_at(t, j, plans, pick):
+        return pick[t * most + j] % crops
 
     return pl.pallas_call(
-        inner,
+        render_kernel,
         out_shape=(
             jax.ShapeDtypeStruct((n, tile_rows + RIM_ROWS, tile_cols), jnp.bfloat16),
             jax.ShapeDtypeStruct((crops, 8, size), jnp.float32),
         ),
         grid_spec=pltpu.PrefetchScalarGridSpec(
-            num_scalar_prefetch=3,
+            num_scalar_prefetch=2,
             grid=(n, most),
             in_specs=[
                 pl.BlockSpec(memory_space=pltpu.SMEM),
@@ -465,7 +464,7 @@
             dimension_semantics=("arbitrary", "arbitrary"), vmem_limit_bytes=VMEM_BYTES
         ),
         name="render",
-    )(plans, pick, used, light, tiles, resample, observed)
+    )(plans, pick, light, tiles, resample, observed)
 
 
 def scatter_kernel(
@@ -677,16 +676,17 @@
     sun_table = sun_vectors(sun_azimuth[0], sun_elevation[0])
     light = jnp.concatenate([sun_table, jnp.exp(exposure)])
     slot_ids = jnp.arange(slot_count, dtype=jnp.int32)
-    reached = jnp.where(receive[None, :] <= slot_ids[:, None], receive[None, :], -1)
-    pick = jnp.argmax(reached, axis=1).astype(jnp.int32)
-    used = (jnp.max(reached, axis=1) == slot_ids).astype(jnp.int32)
+    keys = receive * crops + jnp.arange(crops, dtype=jnp.int32)
+    latest = jnp.max(jnp.where(receive[None, :] <= slot_ids[:, None], keys[None, :], 0), axis=1)
+    filled = jnp.where(jnp.any(receive[None, :] == slot_ids[:, None], axis=1), crops, 0)
+    pick = latest % crops + filled
     plan_by_dest = jnp.pad(
         send_plan[0, 0, 0:2].reshape(2, n, most).transpose(1, 0, 2),
         ((0, 0), (0, 6), (0, 128 - most)),
     )
 
     tiles, plans, smooth = gather_tiles(heights, albedo, plan_by_dest, n, n_dx)
-    tile_grads, sums = render(plans, pick, used, light, tiles, resample, observed, most)
+    tile_grads, sums = render(plans, pick, light, tiles, resample, observed, most)
     height_gradient, camera = scatter_sums(
         tile_grads, sums.reshape(n, crops // n, 8, size), smooth, n, n_dx
     )

time: 150 us -> 146 us (0.973)
  Pallas kernels: 138 us -> 135 us
    pallas_call x1, Pallas kernels: 54 us -> 50 us  [gather_tiles(): pl.pallas_call(functools.partial(gather_kernel, n, n_dx, copies), out_sha...]
    pallas_call x1, Pallas kernels: 31 us -> 32.5 us  [scatter_sums(): pl.pallas_call(functools.partial(scatter_kernel, n, n_dx), out_shape=(jax...]
where the time goes in v4:
time: 146 us
  Pallas kernels  135 us (92%)
  local copies, waits for them, and re-layouts  5.67 us (4%)
  other arithmetic  4.89 us (3%)
    pallas_call x1, Pallas kernels, render(): pl.pallas_call(render_kernel, out_shape=(jax.ShapeDtypeStruct((n, tile_ro...  52 us
    pallas_call x1, Pallas kernels, gather_tiles(): pl.pallas_call(functools.partial(gather_kernel, n, n_dx, copies), out_sha...  50 us
    pallas_call x1, Pallas kernels, scatter_sums(): pl.pallas_call(functools.partial(scatter_kernel, n, n_dx), out_shape=(jax...  32.5 us

profile of v4, /device:TPU:0, one launch (start us, length us, event | category | flops | bytes accessed | tf_op | source)
XLA Modules:
  0.0 145.7 jit_solution(13831549248327987244)
XLA Ops:
  0.6 0.7 fusion.3
  1.3 0.7 cosine_multiply_fusion
  2.0 0.7 exp.3
  2.7 0.6 pad_maximum_fusion.light
  3.3 0.7 slice.24
  4.0 0.1 reshape_squeeze.3
  4.1 0.6 pad.4.plan_ref
  4.7 50.0 %gather_tiles.1 = (s16[8,1040,512]{2,1,0:T(8,128)(2,1)}, s32[8,8,128]{2,1,0:T(8,128)}, f32[512,512]{1,0:T(8,128)}) custom-call(f32[512,512]{1,0:T(8,128)} %heights_ref.1, f32[512,512]{1,0:T(8,128)} %albedo_ref.1, s32[8,8,128]{2,1,0:T(8,128)} %pad.4.plan_ref), custom_call_target="tpu_custom_call" | custom-call | tf_op jit(solution)/shard_map/gather_tiles/pallas_call | solution.py:290
  54.7 0.7 iota_add_fusion
  55.4 0.7 select_reduce_fusion
  56.1 0.7 fusion
  56.9 0.5 fusion.1.pick
  57.4 52.0 %render.1 = (bf16[8,528,512]{2,1,0:T(8,128)(2,1)}, f32[16,8,384]{2,1,0:T(8,128)}) custom-call(s32[8,8,128]{2,1,0:T(8,128)} %get-tuple-element.9.plans, s32[24]{0:T(128)} %fusion.1.pick, f32[4,16]{1,0:T(4,128)} %pad_maximum_fusion.light, s16[8,1040,512]{2,1,0:T(8,128)(2,1)} %get-tuple-element.10.tile_ref, bf16[16,2,384,384]{3,2,1,0:T(8,128)(2,1)} %mats_ref.1, ...), custom_call_target="tpu_custom_call" | custom-call | tf_op jit(solution)/shard_map/render/pallas_call | solution.py:439
  109.4 32.5 %scatter_sums.1 = (f32[512,512]{1,0:T(8,128)}, f32[2,8,384]{2,1,0:T(8,128)}) custom-call(bf16[8,528,512]{2,1,0:T(8,128)(2,1)} %get-tuple-element.11.grads_ref, f32[8,2,8,384]{3,2,1,0:T(8,128)} %bitcast.7, f32[512,512]{1,0:T(8,128)} %get-tuple-element.13.smooth_ref), custom_call_target="tpu_custom_call" | custom-call | tf_op jit(solution)/shard_map/scatter_sums/pallas_call | solution.py:638
  141.9 0.8 multiply_reduce_fusion
  142.7 0.1 slice_multiply_fusion
  142.8 0.7 stack.2
  143.5 2.3 %copy.17 = f32[512,512]{1,0:T(8,128)} copy(f32[512,512]{1,0:T(8,128)} %get-tuple-element.33) | data formatting | bytes 2097152
  (2 shorter events, 0.0 us)
